TPU v7x, 32 devices: a whole 2x2x4 slice. The times are simulated.
32 devices in a mesh: rows: 16 (over z, x, core), rep: 2 (over y).
Axes of the slice: x: 2, y: 2, z: 4, core: 2. Of those that a mesh axis runs over, the one named last changes fastest.
Arguments:
- features: bfloat16 [12288, 256], P('rows'), may hold values from -6 to 6
- tiles: bfloat16 [96, 12, 128, 128], P('rows', 'rep'), may hold values from -0.21875 to 0.21875
- columns: int32 [96, 12], P('rows', 'rep'), may hold values from 0 to 95, as said below
- live: int32 [96, 2], P('rows', 'rep'), may hold values from 1 to 6, as said below
- weight: bfloat16 [256, 256], replicated, may hold values from -0.375 to 0.375
- bias: float32 [256], replicated, may hold values from -3 to 3
- cotangent: bfloat16 [12288, 256], P('rows'), may hold values from -6 to 6
Outputs:
- activations: bfloat16 [12288, 256], P('rows')
- feature_grad: bfloat16 [12288, 256], P('rows')
- weight_grad: float32 [256, 256], replicated
- bias_grad: float32 [256], replicated
Inputs may be any that keep to these rules, and one draw needn't show every extreme that they name: `columns`: the 12 slots of row block g name, in some order, each of the blocks s to s + 2 * 6 - 1 once, where s = g - 6 clipped to 0 .. 84. `live`: 1 to 6 live slots in each half of a row block's slots; some row block in every draw has all 6 live in its first half.
All inputs are finite; a program needn't handle non-finite values.
Results may differ from a plain program's by a relative error of at most 0.0061.
Values may be sent and summed in bfloat16 or wider, within the bound.
A program may use at most 64 MiB of HBM per device.

v0:
```python
import math

import jax
import jax.numpy as jnp
from jax import lax
from jax.sharding import PartitionSpec as P


def extended(block, sides, width):
    for axis, dim in sides:
        count = lax.axis_size(axis)
        forward = [(i, i + 1) for i in range(count - 1)]
        backward = [(target, source) for source, target in forward]
        low = lax.ppermute(
            lax.slice_in_dim(block, block.shape[dim] - width, None, axis=dim), axis, forward
        )
        high = lax.ppermute(lax.slice_in_dim(block, 0, width, axis=dim), axis, backward)
        block = jnp.concatenate([low, block, high], axis=dim)
    return block


def from_behind(x, axis, by):
    count = lax.axis_size(axis)
    pairs = [(i, i + by) for i in range(count) if 0 <= i + by < count]
    return lax.ppermute(x, axis, pairs)


def dense_part(aggregated, grad_input, weight, bias):
    pre_act = jnp.dot(aggregated, weight, preferred_element_type=jnp.float32) + bias
    outputs = jax.nn.silu(pre_act).astype(jnp.bfloat16)
    sigmoid_pre = jax.nn.sigmoid(pre_act)
    pre_grad = (
        grad_input.astype(jnp.float32) * sigmoid_pre * (1.0 + pre_act * (1.0 - sigmoid_pre))
    ).astype(jnp.bfloat16)
    agg_grad = jnp.dot(pre_grad, weight.T, preferred_element_type=jnp.float32).astype(jnp.bfloat16)
    return (outputs, pre_grad, agg_grad)


def local(features, tiles, columns, live, weight, bias, cotangent):
    num_blocks = tiles.shape[0]
    slot_count = tiles.shape[1]
    tile_size = tiles.shape[2]
    feat_width = features.shape[1]
    rows_here = num_blocks * tile_size
    half_rows = rows_here // 2
    row_index = lax.axis_index("rows")
    partner = lax.axis_index("rep")
    node_count = rows_here * lax.axis_size("rows")
    padded = extended(features, (("rows", 0),), rows_here)
    padded_blocks = padded.reshape(3 * num_blocks, tile_size, feat_width)
    local_cols = columns - (row_index - 1) * num_blocks
    live_mask = jnp.arange(slot_count, dtype=jnp.int32)[None, :] < live
    targets = jnp.arange(3 * num_blocks, dtype=jnp.int32)
    selector = (local_cols[:, :, None] == targets[None, None, :]) & live_mask[:, :, None]
    selector = selector.astype(jnp.bfloat16)
    band_tiles = jnp.einsum(
        "bks,bkij->bsij", selector, tiles, preferred_element_type=jnp.float32
    ).astype(jnp.bfloat16)
    partial_sum = jnp.einsum(
        "bsij,sjf->bif", band_tiles, padded_blocks, preferred_element_type=jnp.float32
    )
    partial_sum = partial_sum.reshape(rows_here, feat_width)
    aggregate = lax.psum(partial_sum, "rep").astype(jnp.bfloat16)
    activations, pre_grad, agg_grad = dense_part(aggregate, cotangent, weight, bias)
    agg_half = lax.dynamic_slice_in_dim(aggregate, partner * half_rows, half_rows, 0)
    grad_half = lax.dynamic_slice_in_dim(pre_grad, partner * half_rows, half_rows, 0)
    weight_part = lax.dot_general(
        agg_half, grad_half, (((0,), (0,)), ((), ())), preferred_element_type=jnp.float32
    )
    bias_part = jnp.sum(grad_half.astype(jnp.float32), axis=0)
    weight_total, bias_total = lax.psum((weight_part, bias_part), ("rows", "rep"))
    scale = 1.0 / math.sqrt(node_count)
    weight_grad = weight_total * scale
    bias_grad = bias_total * scale
    grad_blocks = agg_grad.reshape(num_blocks, tile_size, feat_width)
    spread = jnp.einsum(
        "bsij,bif->sjf", band_tiles, grad_blocks, preferred_element_type=jnp.float32
    )
    from_above = from_behind(spread[:num_blocks], "rows", -1)
    from_below = from_behind(spread[2 * num_blocks :].astype(jnp.bfloat16), "rows", 1).astype(
        jnp.float32
    )
    own_terms = spread[num_blocks : 2 * num_blocks] + from_above + from_below
    own_total = lax.psum(own_terms, "rep")
    feature_grad = own_total.reshape(rows_here, feat_width).astype(jnp.bfloat16)
    return (activations, feature_grad, weight_grad, bias_grad)


def solution(mesh):
    placed = (
        P("rows", None),
        P("rows", "rep", None, None),
        P("rows", "rep"),
        P("rows", "rep"),
        P(),
        P(),
        P("rows", None),
    )
    return jax.shard_map(
        local,
        mesh=mesh,
        in_specs=placed,
        out_specs=(P("rows", None), P("rows", None), P(), P()),
        check_vma=False,
    )
```

profile of v0, /device:TPU:0, one launch (start us, length us, event | category | flops | bytes accessed | tf_op | source)
XLA Modules:
  0.0 218.3 jit_solution(8993651444586286694)
XLA Ops:
  7.2 0.0 copy-start
  7.2 0.0 all-reduce.4.cloned.1.call-start
  7.2 2.5 %collective-permute-start = (bf16[768,256]{1,0:T(8,128)(2,1)}, bf16[768,256]{1,0:T(8,128)(2,1)S(1)}, u32[]{:S(2)}, u32[]{:S(2)}) collective-permute-start(bf16[768,256]{1,0:T(8,128)(2,1)} %param.7), channel_id=1, source_target_pairs={{0,2},{2,4},{4,6},{6,8},{8,10},{10,12},{12,14},{14,16},{16,18},{18... | collective-permute-start | bytes 1179656 | tf_op jit(solution)/shard_map/ppermute | solution.py:14
  9.7 1.3 collective-permute-start.1
  11.1 0.7 broadcast_subtract_fusion
  11.7 0.7 iota_compare_fusion.1
  12.5 0.0 copy-done
  12.5 0.0 copy-start.5
  12.5 2.2 %convolution_convert_fusion = bf16[6,18,128,128]{3,1,2,0:T(8,128)(2,1)S(1)} fusion(bf16[6,6,128,128]{3,2,1,0:T(8,128)(2,1)S(1)} %copy-done, s32[6,6]{1,0:T(8,128)S(1)} %broadcast_subtract_fusion, pred[6,6]{1,0:T(8,128)(4,1)S(1)} %iota_compare_fusion.1), kind=kOutput, calls=%fused_computation.4 | convolution fusion | flops 23004432 | bytes 4718772 | tf_op jit(solution)/shard_map/bks,bkij->bsij/dot_general | solution.py:56
  14.7 0.0 copy-start.1
  14.7 0.0 collective-permute-done
  14.7 0.9 collective-permute-done.1
  15.7 0.0 copy-done.5
  15.7 0.1 pad_maximum_fusion
  15.7 1.1 copy-done.1
  16.8 0.0 copy-start.6
  16.8 0.0 copy-start.7
  16.8 1.1 fusion.8
  17.9 20.1 %all-reduce.5 = bf16[768,256]{1,0:T(8,128)(2,1)S(1)} all-reduce(f32[768,256]{1,0:T(8,128)S(1)} %fusion.8), channel_id=1, replica_groups=mesh['rows'=16,'rep'=2] {'rep'}, use_global_device_ids=true, to_apply=%region_0.0 | all-reduce | flops 196608 | bytes 1179648 | tf_op jit(solution)/shard_map/psum | solution.py:63
  38.0 0.0 copy-done.6
  38.1 0.0 copy-done.7
  38.1 0.0 copy-start.4
  38.1 0.0 copy-start.2
  38.1 2.5 %multiply_convert_fusion = (bf16[768,256]{1,0:T(8,128)(2,1)S(1)}, bf16[768,256]{1,0:T(8,128)(2,1)}) fusion(bf16[768,256]{1,0:T(8,128)(2,1)} %param.13, f32[256]{0:T(256)S(1)} %copy-done.7, bf16[768,256]{1,0:T(8,128)(2,1)S(1)} %all-reduce.5, bf16[256,256]{1,0:T(8,128)(2,1)S(1)} %copy-done.6), kind=kOutput, calls=%fused_computation.14 | convolution fusion | flops 103219200 | bytes 1704960 | tf_op jit(solution)/shard_map/dot_general | solution.py:29
  40.5 0.0 copy-done.4
  40.6 0.0 copy-start.3
  40.6 0.3 convolution_convert_fusion.1
  40.8 0.5 copy-done.3
  41.3 0.0 copy-done.2
  41.3 1.2 fusion.4
  42.5 1.0 slice.14
  43.5 1.3 collective-permute-start.2
  44.8 0.8 slice.20
  45.5 2.0 fusion.12
  47.5 0.0 all-reduce.4.cloned.1.call-update
  47.6 7.0 %collective-permute-start.3 = (bf16[6,128,256]{2,1,0:T(8,128)(2,1)}, bf16[6,128,256]{2,1,0:T(8,128)(2,1)}, u32[]{:S(2)}, u32[]{:S(2)}) collective-permute-start(bf16[6,128,256]{2,1,0:T(8,128)(2,1)} %slice.20), channel_id=1, source_target_pairs={{0,2},{2,4},{4,6},{6,8},{8,10},{10,12},{12,14},{14,16},{16,18},{18... | collective-permute-start | bytes 1179656 | tf_op jit(solution)/shard_map/ppermute | solution.py:25
  54.6 1.0 convert_reduce_fusion
  55.5 48.5 %psum.31 = f32[256]{0:T(256)S(1)} all-reduce(f32[256]{0:T(256)S(1)} %convert_reduce_fusion), channel_id=1, replica_groups=mesh['rows'=16,'rep'=2] {'rows','rep'}, use_global_device_ids=true, to_apply=%region_4.5 | all-reduce | flops 256 | bytes 2048 | tf_op jit(solution)/shard_map/psum | solution.py:71
  104.0 0.6 broadcast_multiply_fusion.1
  104.6 80.3 %all-reduce.4.cloned.1.call-done = f32[256,256]{1,0:T(8,128)} async-done(((f32[256,256]{1,0:T(8,128)}), f32[256,256]{1,0:T(8,128)}) %all-reduce.4.cloned.1.call-update) | async-done | bytes 262160 | tf_op jit(solution)/shard_map/psum | solution.py:71
  184.9 1.7 broadcast_multiply_fusion
  186.5 0.0 collective-permute-done.3
  186.6 0.0 collective-permute-done.2
  186.6 2.3 %fusion.11 = f32[6,128,256]{2,1,0:T(8,128)} fusion(f32[6,128,256]{2,1,0:T(8,128)} %collective-permute-done.2, f32[18,128,256]{2,1,0:T(8,128)S(1)} %fusion.4, bf16[6,128,256]{2,1,0:T(8,128)(2,1)} %collective-permute-done.3), kind=kLoop, calls=%fused_computation.13 | loop fusion | flops 589824 | bytes 2752512 | tf_op jit(solution)/shard_map/add | solution.py:83
  188.8 22.7 %all-reduce.6 = bf16[6,128,256]{2,1,0:T(8,128)(2,1)} all-reduce(f32[6,128,256]{2,1,0:T(8,128)} %fusion.11), channel_id=1, replica_groups=mesh['rows'=16,'rep'=2] {'rep'}, use_global_device_ids=true, to_apply=%region_1.2 | all-reduce | flops 196608 | bytes 1179648 | tf_op jit(solution)/shard_map/psum | solution.py:84
Async XLA Ops:
  7.2 5.3 %copy-start = (bf16[6,6,128,128]{3,2,1,0:T(8,128)(2,1)S(1)}, bf16[6,6,128,128]{3,2,1,0:T(8,128)(2,1)}, u32[]{:S(2)}) copy-start(bf16[6,6,128,128]{3,2,1,0:T(8,128)(2,1)} %param.8) | copy-start | bytes 3538948
  7.2 177.7 %all-reduce.4.cloned.1.call-start = ((), (), s32[]{:S(2)}) async-start(), calls=%async_computation | async-start | bytes 524288 | tf_op jit(solution)/shard_map/psum | solution.py:71
  7.2 7.5 %collective-permute-start = (bf16[768,256]{1,0:T(8,128)(2,1)}, bf16[768,256]{1,0:T(8,128)(2,1)S(1)}, u32[]{:S(2)}, u32[]{:S(2)}) collective-permute-start(bf16[768,256]{1,0:T(8,128)(2,1)} %param.7), channel_id=1, source_target_pairs={{0,2},{2,4},{4,6},{6,8},{8,10},{10,12},{12,14},{14,16},{16,18},{18... | collective-permute-start | bytes 1179656 | tf_op jit(solution)/shard_map/ppermute | solution.py:14
  9.7 5.9 %collective-permute-start.1 = (bf16[768,256]{1,0:T(8,128)(2,1)}, bf16[768,256]{1,0:T(8,128)(2,1)S(1)}, u32[]{:S(2)}, u32[]{:S(2)}) collective-permute-start(bf16[768,256]{1,0:T(8,128)(2,1)} %param.7), channel_id=1, source_target_pairs={{2,0},{4,2},{6,4},{8,6},{10,8},{12,10},{14,12},{16,14},{18,16},{20... | collective-permute-start | bytes 1179656 | tf_op jit(solution)/shard_map/ppermute | solution.py:17
  12.5 3.2 %copy-start.5 = (bf16[768,256]{1,0:T(8,128)(2,1)S(1)}, bf16[768,256]{1,0:T(8,128)(2,1)}, u32[]{:S(2)}) copy-start(bf16[768,256]{1,0:T(8,128)(2,1)} %param.7) | copy-start | bytes 1179652
  14.7 2.1 copy-start.1
  16.8 21.2 %copy-start.6 = (bf16[256,256]{1,0:T(8,128)(2,1)S(1)}, bf16[256,256]{1,0:T(8,128)(2,1)}, u32[]{:S(2)}) copy-start(bf16[256,256]{1,0:T(8,128)(2,1)} %param.11) | copy-start | bytes 393220
  16.8 21.2 %copy-start.7 = (f32[256]{0:T(256)S(1)}, f32[256]{0:T(256)}, u32[]{:S(2)}) copy-start(f32[256]{0:T(256)} %param.12) | copy-start | bytes 3076
  38.1 2.5 %copy-start.4 = (bf16[768,256]{1,0:T(8,128)(2,1)}, bf16[768,256]{1,0:T(8,128)(2,1)S(1)}, u32[]{:S(2)}) copy-start(bf16[768,256]{1,0:T(8,128)(2,1)S(1)} %all-reduce.5) | copy-start | bytes 1179652
  38.1 3.2 %copy-start.2 = (bf16[6,18,128,128]{3,1,2,0:T(8,128)(2,1)S(1)}, bf16[6,18,128,128]{3,1,2,0:T(8,128)(2,1)}, u32[]{:S(2)}) copy-start(bf16[6,18,128,128]{3,1,2,0:T(8,128)(2,1)} %copy-done.1) | copy-start | bytes 10616836
  40.6 0.8 copy-start.3
  43.5 143.1 %collective-permute-start.2 = (f32[6,128,256]{2,1,0:T(8,128)}, f32[6,128,256]{2,1,0:T(8,128)}, u32[]{:S(2)}, u32[]{:S(2)}) collective-permute-start(f32[6,128,256]{2,1,0:T(8,128)} %slice.14), channel_id=1, source_target_pairs={{2,0},{4,2},{6,4},{8,6},{10,8},{12,10},{14,12},{16,14},{18,16},{20... | collective-permute-start | bytes 2359304 | tf_op jit(solution)/shard_map/ppermute | solution.py:25
  47.6 139.0 %collective-permute-start.3 = (bf16[6,128,256]{2,1,0:T(8,128)(2,1)}, bf16[6,128,256]{2,1,0:T(8,128)(2,1)}, u32[]{:S(2)}, u32[]{:S(2)}) collective-permute-start(bf16[6,128,256]{2,1,0:T(8,128)(2,1)} %slice.20), channel_id=1, source_target_pairs={{0,2},{2,4},{4,6},{6,8},{8,10},{10,12},{12,14},{14,16},{16,18},{18... | collective-permute-start | bytes 1179656 | tf_op jit(solution)/shard_map/ppermute | solution.py:25
Sparse Core Ops, SparseCore 0:
  47.7 137.1 all-reduce.3
where the time goes:
time: 219 us; the launch traced here: 218 us
  blocking collectives  91.3 us (42%)
  waiting for transfers between devices  81.2 us (37%)
  between operations  14.2 us (6%)
  starting transfers between devices  12.1 us (6%)
  matrix products  9.22 us (4%)
  other arithmetic  6.98 us (3%)
  local copies, waits for them, and re-layouts  3.34 us (2%)
    psum x1, waiting for transfers between devices, local(): lax.psum((weight_part, bias_part), ('rows', 'rep'))  80.3 us
    psum x1, blocking collectives, local(): lax.psum((weight_part, bias_part), ('rows', 'rep'))  48.5 us
    psum x1, blocking collectives, local(): own_total = lax.psum(own_terms, 'rep')  22.7 us
    psum x1, blocking collectives, local(): aggregate = lax.psum(partial_sum, 'rep').astype(jnp.bfloat16)  20.1 us
    ppermute x2, starting transfers between devices, from_behind(): return lax.ppermute(x, axis, pairs)  8.27 us
  transfers between devices with their start and end apart: 5, of which 2 were waited for; matrix products, arithmetic and copies ran while one was open for 4% of the time, Pallas kernels for 0%

commit v1 on v0

v1 whole, which is shorter than its diff:
```python
import functools
import math

import jax
import jax.numpy as jnp
from jax import lax
from jax.experimental import pallas as pl
from jax.experimental.pallas import tpu as pltpu
from jax.sharding import PartitionSpec as P

MESH = pl.DeviceIdType.MESH
PLANE = 4
F32, BF16 = jnp.float32, jnp.bfloat16
NT = (((1,), (1,)), ((), ()))
TN = (((0,), (0,)), ((), ()))


def remote(src, dst, send_sem, recv_sem, device):
    return pltpu.make_async_remote_copy(
        src_ref=src, dst_ref=dst, send_sem=send_sem, recv_sem=recv_sem,
        device_id=device, device_id_type=MESH,
    )


def kernel(
    n, scale,
    cols_ref, live_ref, feat_hbm, tiles_hbm, w_ref, b_ref, cot_hbm,
    act_ref, fg_ref, wg_ref, bg_ref,
    feat, tiles, tiles_t, band, band_t, cot, eff, acc,
    p_send, p_recv, agg_grad, s_send, s_recv, t_send, t_recv,
    w_send, w_recv, z_recv, g_send, g_recv,
    local_sem, f_ssem, f_rsem, p_ssem, p_rsem, s_ssem, s_rsem, t_ssem, t_rsem,
    w_ssem, w_rsem, z_ssem, z_rsem, g_ssem, g_rsem,
):
    me, rep = lax.axis_index("rows"), lax.axis_index("rep")
    nb, slots, tile = tiles_hbm.shape[0], tiles_hbm.shape[1], tiles_hbm.shape[2]
    rows = nb * tile
    width = w_ref.shape[0]
    groups = n // PLANE
    quad = lax.rem(me, PLANE)
    layer = lax.div(me, PLANE)
    has_low, has_high = me > 0, me < n - 1
    low, high = (me - 1, rep), (me + 1, rep)
    partner = (me, 1 - rep)
    chunk = 2 * tile
    chunks = rows // chunk

    def plane_peer(d):
        return lax.rem(quad + d, PLANE)

    def layer_peer(d):
        return lax.rem(layer + d, groups)

    barrier = pltpu.get_barrier_semaphore()

    def greet(device):
        pl.semaphore_signal(barrier, inc=1, device_id=device, device_id_type=MESH)

    @pl.when(has_low)
    def _():
        greet(low)

    @pl.when(has_high)
    def _():
        greet(high)

    greet(partner)
    for d in range(1, PLANE):
        greet((layer * PLANE + plane_peer(d), rep))
    for d in range(1, groups):
        greet((layer_peer(d) * PLANE + quad, rep))

    tiles_in = pltpu.make_async_copy(
        tiles_hbm, tiles.at[pl.ds(0, nb)], local_sem.at[0]
    )
    feat_in = pltpu.make_async_copy(feat_hbm, feat.at[1], local_sem.at[1])
    cot_in = pltpu.make_async_copy(cot_hbm, cot, local_sem.at[2])
    tiles_in.start()
    feat_in.start()
    cot_in.start()

    pl.semaphore_wait(
        barrier, PLANE + groups - 1 + has_low.astype(jnp.int32) + has_high.astype(jnp.int32)
    )

    def feat_copy(j, up):
        piece = pl.ds(j * chunk, chunk)
        return remote(
            feat_hbm.at[piece], feat.at[0 if up else 2, piece],
            f_ssem.at[int(up), j], f_rsem.at[int(up), j], high if up else low,
        )

    @pl.when(has_high)
    def _():
        for j in range(chunks):
            feat_copy(j, True).start()

    @pl.when(has_low)
    def _():
        for j in range(chunks):
            feat_copy(j, False).start()

    @pl.when(jnp.logical_not(has_low))
    def _():
        feat[0] = jnp.zeros(feat.shape[1:], BF16)
        s_recv[0] = jnp.zeros(s_recv.shape[1:], BF16)

    @pl.when(jnp.logical_not(has_high))
    def _():
        feat[2] = jnp.zeros(feat.shape[1:], BF16)
        s_recv[1] = jnp.zeros(s_recv.shape[1:], BF16)

    first = (me - 1) * nb
    for g in range(nb):
        count = live_ref[g, 0]
        for k in range(slots):
            eff[g * slots + k] = jnp.where(k < count, cols_ref[g, k] - first, -1)

    tiles[nb, 0] = jnp.zeros((tile, tile), BF16)
    tiles_t[nb, 0] = jnp.zeros((tile, tile), BF16)
    tiles_in.wait()

    def flip(g, carry):
        for k in range(slots):
            tiles_t[g, k] = tiles[g, k].T
        return carry

    lax.fori_loop(0, nb, flip, 0)

    def place(s, carry):
        at = pl.ds(pl.multiple_of(s * tile, tile), tile)
        for g in range(nb):
            a, k_at = jnp.int32(nb), jnp.int32(0)
            for k in range(slots):
                hit = eff[g * slots + k] == s
                a = jnp.where(hit, g, a)
                k_at = jnp.where(hit, k, k_at)
            band[g * tile:(g + 1) * tile, at] = tiles[a, k_at]
            band_t[at, g * tile:(g + 1) * tile] = tiles_t[a, k_at]
        return carry

    lax.fori_loop(0, 3 * nb, place, 0)
    feat_in.wait()

    def dot(a, b):
        return jnp.dot(a, b, preferred_element_type=F32)

    def own_rows(m, carry):
        at = pl.ds(pl.multiple_of(m * chunk, chunk), chunk)
        acc[at, :] = dot(band[at, rows:2 * rows], feat[1])
        return carry

    lax.fori_loop(0, chunks, own_rows, 0)

    @pl.when(has_low)
    def _():
        for j in range(chunks):
            feat_copy(j, True).wait_recv()

    def low_rows(m, carry):
        at = pl.ds(pl.multiple_of(m * chunk, chunk), chunk)
        acc[at, :] += dot(band[at, :rows], feat[0])
        return carry

    lax.fori_loop(0, chunks, low_rows, 0)

    @pl.when(has_high)
    def _():
        for j in range(chunks):
            feat_copy(j, False).wait_recv()

    def p_copy(m):
        return remote(p_send.at[m], p_recv.at[m], p_ssem.at[m], p_rsem.at[m], partner)

    for m in range(chunks):
        at = pl.ds(m * chunk, chunk)
        p_send[m] = (acc[at, :] + dot(band[at, 2 * rows:], feat[2])).astype(BF16)
        p_copy(m).start()
    cot_in.wait()

    w = w_ref[...]
    w_part = jnp.zeros((width, width), F32)
    b_part = jnp.zeros((1, width), F32)
    for m in range(chunks):
        at = pl.ds(m * chunk, chunk)
        p_copy(m).wait_recv()
        agg = (p_send[m].astype(F32) + p_recv[m].astype(F32)).astype(BF16)
        pre = dot(agg, w) + b_ref[...]
        sig = jax.nn.sigmoid(pre)
        act_ref[at, :] = (pre * sig).astype(BF16)
        pre_grad = (cot[at, :].astype(F32) * sig * (1.0 + pre * (1.0 - sig))).astype(BF16)
        agg_grad[at, :] = lax.dot_general(
            pre_grad, w, NT, preferred_element_type=F32
        ).astype(BF16)
        w_part += lax.dot_general(agg, pre_grad, TN, preferred_element_type=F32)
        b_part += jnp.sum(pre_grad.astype(F32), axis=0, keepdims=True)

    part = width // PLANE
    for c in range(PLANE):
        w_send[c, :part] = w_part[c * part:(c + 1) * part].astype(BF16)
        w_send[c, part:] = jnp.broadcast_to(b_part, (16, width)).astype(BF16)

    def w_copy(d, slot):
        peer = plane_peer(d)
        return remote(
            w_send.at[peer], w_recv.at[slot], w_ssem.at[d - 1], w_rsem.at[d - 1],
            (layer * PLANE + peer, rep),
        )

    for d in range(1, PLANE):
        w_copy(d, quad).start()
    w_recv[quad] = w_send[quad]

    def s_copy(j, up):
        return remote(
            s_send.at[int(up), j], s_recv.at[1 - int(up) if not up else 0, j],
            s_ssem.at[int(up), j], s_rsem.at[int(up), j], high if up else low,
        )

    for j in range(chunks):
        s_send[1, j] = dot(
            band_t[2 * rows + j * chunk:2 * rows + (j + 1) * chunk, :], agg_grad[...]
        ).astype(BF16)

        @pl.when(has_high)
        def _():
            s_copy(j, True).start()

        s_send[0, j] = dot(
            band_t[j * chunk:(j + 1) * chunk, :], agg_grad[...]
        ).astype(BF16)

        @pl.when(has_low)
        def _():
            s_copy(j, False).start()

    for d in range(1, PLANE):
        w_copy(d, lax.rem(quad + PLANE - d, PLANE)).wait_recv()
    z_recv[layer] = sum(w_recv[c].astype(F32) for c in range(PLANE)).astype(BF16)

    def z_copy(d, slot):
        return remote(
            z_recv.at[layer], z_recv.at[slot], z_ssem.at[d - 1], z_rsem.at[d - 1],
            (layer_peer(d) * PLANE + quad, rep),
        )

    for d in range(1, groups):
        z_copy(d, layer).start()

    def own_terms(m, carry):
        at = pl.ds(pl.multiple_of(m * chunk, chunk), chunk)
        own = pl.ds(pl.multiple_of(rows + m * chunk, chunk), chunk)
        acc[at, :] = dot(band_t[own, :], agg_grad[...])
        return carry

    lax.fori_loop(0, chunks, own_terms, 0)

    def t_copy(m):
        return remote(t_send.at[m], t_recv.at[m], t_ssem.at[m], t_rsem.at[m], partner)

    for m in range(chunks):
        @pl.when(has_low)
        def _():
            s_copy(m, True).wait_recv()

        @pl.when(has_high)
        def _():
            s_copy(m, False).wait_recv()

        t_send[m] = (
            acc[m * chunk:(m + 1) * chunk, :] + s_recv[0, m].astype(F32) + s_recv[1, m].astype(F32)
        ).astype(BF16)
        t_copy(m).start()

    for d in range(1, groups):
        z_copy(d, lax.rem(layer + groups - d, groups)).wait_recv()
    total = sum(z_recv[c].astype(F32) for c in range(groups)) * scale
    bg_ref[...] = total[part:part + 1]
    g_send[...] = total[:part]
    g_recv[quad] = total[:part]

    def g_copy(d, slot):
        return remote(
            g_send, g_recv.at[slot], g_ssem.at[d - 1], g_rsem.at[d - 1],
            (layer * PLANE + plane_peer(d), rep),
        )

    for d in range(1, PLANE):
        g_copy(d, quad).start()

    for m in range(chunks):
        t_copy(m).wait_recv()
        fg_ref[m * chunk:(m + 1) * chunk, :] = (
            t_send[m].astype(F32) + t_recv[m].astype(F32)
        ).astype(BF16)

    for d in range(1, PLANE):
        g_copy(d, lax.rem(quad + PLANE - d, PLANE)).wait_recv()
    for c in range(PLANE):
        wg_ref[c * part:(c + 1) * part, :] = g_recv[c]

    @pl.when(has_high)
    def _():
        for j in range(chunks):
            feat_copy(j, True).wait_send()
            s_copy(j, True).wait_send()

    @pl.when(has_low)
    def _():
        for j in range(chunks):
            feat_copy(j, False).wait_send()
            s_copy(j, False).wait_send()

    for m in range(chunks):
        p_copy(m).wait_send()
        t_copy(m).wait_send()
    for d in range(1, PLANE):
        w_copy(d, quad).wait_send()
        g_copy(d, quad).wait_send()
    for d in range(1, groups):
        z_copy(d, layer).wait_send()


def solution(mesh):
    n = mesh.shape["rows"]

    def local(features, tiles, columns, live, weight, bias, cotangent):
        nb, slots, tile, _ = tiles.shape
        rows, width = features.shape
        chunk = 2 * tile
        chunks = rows // chunk
        groups = n // PLANE
        part = width // PLANE
        vmem, dma = pltpu.VMEM, pltpu.SemaphoreType.DMA
        any_, whole = pl.BlockSpec(memory_space=pl.ANY), pl.BlockSpec(memory_space=pltpu.VMEM)
        smem = pl.BlockSpec(memory_space=pltpu.SMEM)
        act, feature_grad, weight_grad, bias_grad = pl.pallas_call(
            functools.partial(kernel, n, 1.0 / math.sqrt(rows * n)),
            out_shape=(
                jax.ShapeDtypeStruct((rows, width), BF16),
                jax.ShapeDtypeStruct((rows, width), BF16),
                jax.ShapeDtypeStruct((width, width), F32),
                jax.ShapeDtypeStruct((1, width), F32),
            ),
            in_specs=[smem, smem, any_, any_, whole, whole, any_],
            out_specs=(whole, whole, whole, whole),
            scratch_shapes=[
                vmem((3, rows, width), BF16),
                vmem((nb + 1, slots, tile, tile), BF16),
                vmem((nb + 1, slots, tile, tile), BF16),
                vmem((rows, 3 * rows), BF16),
                vmem((3 * rows, rows), BF16),
                vmem((rows, width), BF16),
                pltpu.SMEM((nb * slots,), jnp.int32),
                vmem((rows, width), F32),
                vmem((chunks, chunk, width), BF16),
                vmem((chunks, chunk, width), BF16),
                vmem((rows, width), BF16),
                vmem((2, chunks, chunk, width), BF16),
                vmem((2, chunks, chunk, width), BF16),
                vmem((chunks, chunk, width), BF16),
                vmem((chunks, chunk, width), BF16),
                vmem((PLANE, part + 16, width), BF16),
                vmem((PLANE, part + 16, width), BF16),
                vmem((groups, part + 16, width), BF16),
                vmem((part, width), F32),
                vmem((PLANE, part, width), F32),
                dma((3,)),
                dma((2, chunks)), dma((2, chunks)),
                dma((chunks,)), dma((chunks,)),
                dma((2, chunks)), dma((2, chunks)),
                dma((chunks,)), dma((chunks,)),
                dma((PLANE - 1,)), dma((PLANE - 1,)),
                dma((groups - 1,)), dma((groups - 1,)),
                dma((PLANE - 1,)), dma((PLANE - 1,)),
            ],
            compiler_params=pltpu.CompilerParams(
                collective_id=0, has_side_effects=True, vmem_limit_bytes=48 * 2**20
            ),
        )(columns, live, features, tiles, weight, bias.reshape(1, width), cotangent)
        return act, feature_grad, weight_grad, bias_grad.reshape(width)

    return jax.shard_map(
        local,
        mesh=mesh,
        in_specs=(
            P("rows", None), P("rows", "rep", None, None), P("rows", "rep"), P("rows", "rep"),
            P(), P(), P("rows", None),
        ),
        out_specs=(P("rows", None), P("rows", None), P(), P()),
        check_vma=False,
    )
```

time: 219 us -> 49.8 us (0.23)
  blocking collectives: 91.3 us -> 0 us
  waiting for transfers between devices: 81.2 us -> 0 us
  Pallas kernels: 0 us -> 39.3 us
  between operations: 14.2 us -> 0.65 us
  starting transfers between devices: 12.1 us -> 0 us
  matrix products: 9.22 us -> 0 us
  other arithmetic: 6.98 us -> 0 us
  local copies, waits for them, and re-layouts: 3.34 us -> 9.03 us
    psum x3 -> x0, blocking collectives: 91.3 us -> none  [the longest x1 48.5 us: local(): lax.psum((weight_part, bias_part), ('rows', 'rep'))]
    psum x1 -> x0, waiting for transfers between devices: 80.3 us -> none  [local(): lax.psum((weight_part, bias_part), ('rows', 'rep'))]
    pallas_call x0 -> x1, Pallas kernels: none -> 39.3 us  [local(): pl.pallas_call(functools.partial(kernel, n, 1.0 / math.sqrt(rows * n)), o...]
    ppermute x4 -> x0, starting transfers between devices: 12.1 us -> none  [the longest x2 8.27 us: from_behind(): return lax.ppermute(x, axis, pairs)]
    dot_general x6 -> x0, matrix products: 9.22 us -> none  [the longest x1 2.46 us: dense_part(): jnp.dot(aggregated, weight, preferred_element_type=jnp.float32) + bias]
    unnamed x16 -> x17, local copies, waits for them, and re-layouts: 1.58 us -> 9.03 us
    add x1 -> x0, other arithmetic: 2.26 us -> none  [local(): own_terms = spread[num_blocks:2 * num_blocks] + from_above + from_below]
    mul x2 -> x0, other arithmetic: 2.24 us -> none  [the longest x1 1.68 us: local(): weight_grad = weight_total * scale]
  transfers between devices with their start and end apart: 5 -> 0, of which waited for: 2 -> 0; matrix products, arithmetic and copies ran while one was open for 4% -> 0% of each run, Pallas kernels for 0% -> 0%
where the time goes in v1:
time: 49.8 us; the launch traced here: 49 us
  Pallas kernels  39.3 us (79%)
  local copies, waits for them, and re-layouts  9.03 us (18%)
  between operations  0.65 us (1%)
    pallas_call x1, Pallas kernels, local(): pl.pallas_call(functools.partial(kernel, n, 1.0 / math.sqrt(rows * n)), o...  39.3 us
    unnamed x17, local copies, waits for them, and re-layouts  9.03 us

profile of v1, /device:TPU:0, one launch (start us, length us, event | category | flops | bytes accessed | tf_op | source)
XLA Modules:
  0.0 49.0 jit_solution(14047684205708807401)
XLA Ops:
  0.6 0.7 %copy.11.live_ref = s32[6,1]{1,0:T(8,128)S(1)} copy(s32[6,1]{0,1:T(1,128)} %param.10) | data formatting | bytes 48 | tf_op args[3]
  1.4 0.0 copy-start
  1.4 1.3 %copy-done = bf16[6,6,128,128]{3,2,1,0:T(8,128)(2,1)S(1)} copy-done((bf16[6,6,128,128]{3,2,1,0:T(8,128)(2,1)S(1)}, bf16[6,6,128,128]{3,2,1,0:T(8,128)(2,1)}, u32[]{:S(2)}) %copy-start) | copy-done | bytes 1179672
  2.6 0.0 copy-start.1
  2.6 1.0 %copy-done.1 = bf16[768,256]{1,0:T(8,128)(2,1)S(1)} copy-done((bf16[768,256]{1,0:T(8,128)(2,1)S(1)}, bf16[768,256]{1,0:T(8,128)(2,1)}, u32[]{:S(2)}) %copy-start.1) | copy-done | bytes 393240
  3.6 0.0 copy-start.2
  3.6 1.0 %copy-done.2 = bf16[768,256]{1,0:T(8,128)(2,1)S(1)} copy-done((bf16[768,256]{1,0:T(8,128)(2,1)S(1)}, bf16[768,256]{1,0:T(8,128)(2,1)}, u32[]{:S(2)}) %copy-start.2) | copy-done | bytes 393240
  4.6 0.0 copy-start.3
  4.6 0.9 %copy-done.3 = bf16[256,256]{1,0:T(8,128)(2,1)S(1)} copy-done((bf16[256,256]{1,0:T(8,128)(2,1)S(1)}, bf16[256,256]{1,0:T(8,128)(2,1)}, u32[]{:S(2)}) %copy-start.3) | copy-done | bytes 131096
  5.5 0.0 copy-start.4
  5.5 0.7 %copy-done.4 = s32[6,6]{1,0:T(8,128)S(1)} copy-done((s32[6,6]{1,0:T(8,128)S(1)}, s32[6,6]{1,0:T(8,128)}, u32[]{:S(2)}) %copy-start.4) | copy-done | bytes 168
  6.2 0.0 copy-start.5
  6.2 0.7 %copy-done.5 = f32[256]{0:T(256)S(1)} copy-done((f32[256]{0:T(256)S(1)}, f32[256]{0:T(256)}, u32[]{:S(2)}) %copy-start.5) | copy-done | bytes 1048
  6.9 39.3 %shard_map.102 = (bf16[768,256]{1,0:T(8,128)(2,1)S(1)}, bf16[768,256]{1,0:T(8,128)(2,1)S(1)}, f32[256,256]{1,0:T(8,128)S(1)}, f32[1,256]{1,0:T(1,128)S(1)}) custom-call(s32[6,6]{1,0:T(8,128)S(1)} %copy-done.4, s32[6,1]{1,0:T(8,128)S(1)} %copy.11.live_ref, bf16[768,256]{1,0:T(8,128)(2,1)S(1)} %copy-done.1, bf16[6,6,128,128]{3,2,1,0:T(8,128)(2,1)S(1)} %copy-done, ...), custom_call_target="tpu_custom_call" | custom-call | tf_op jit(solution)/shard_map/pallas_call | solution.py:337
  46.3 0.7 %copy.16 = bf16[768,256]{1,0:T(8,128)(2,1)} copy(bf16[768,256]{1,0:T(8,128)(2,1)S(1)} %get-tuple-element.16) | data formatting | bytes 786432
  47.0 0.7 %copy.17 = bf16[768,256]{1,0:T(8,128)(2,1)} copy(bf16[768,256]{1,0:T(8,128)(2,1)S(1)} %get-tuple-element.17) | data formatting | bytes 786432
  47.8 0.7 %copy.18 = f32[256,256]{1,0:T(8,128)} copy(f32[256,256]{1,0:T(8,128)S(1)} %get-tuple-element.18) | data formatting | bytes 524288
  48.5 0.6 %copy.19 = f32[256]{0:T(256)} copy(f32[256]{0:T(256)S(1)} %bitcast.3) | data formatting | bytes 2048
Async XLA Ops:
  1.4 1.3 %copy-start = (bf16[6,6,128,128]{3,2,1,0:T(8,128)(2,1)S(1)}, bf16[6,6,128,128]{3,2,1,0:T(8,128)(2,1)}, u32[]{:S(2)}) copy-start(bf16[6,6,128,128]{3,2,1,0:T(8,128)(2,1)} %tiles_hbm.1) | copy-start | bytes 3538948
  2.6 1.0 %copy-start.1 = (bf16[768,256]{1,0:T(8,128)(2,1)S(1)}, bf16[768,256]{1,0:T(8,128)(2,1)}, u32[]{:S(2)}) copy-start(bf16[768,256]{1,0:T(8,128)(2,1)} %feat_hbm.1) | copy-start | bytes 1179652
  3.6 1.0 %copy-start.2 = (bf16[768,256]{1,0:T(8,128)(2,1)S(1)}, bf16[768,256]{1,0:T(8,128)(2,1)}, u32[]{:S(2)}) copy-start(bf16[768,256]{1,0:T(8,128)(2,1)} %cot_hbm.1) | copy-start | bytes 1179652
  4.6 0.9 %copy-start.3 = (bf16[256,256]{1,0:T(8,128)(2,1)S(1)}, bf16[256,256]{1,0:T(8,128)(2,1)}, u32[]{:S(2)}) copy-start(bf16[256,256]{1,0:T(8,128)(2,1)} %w_ref.1) | copy-start | bytes 393220
  5.5 0.7 %copy-start.4 = (s32[6,6]{1,0:T(8,128)S(1)}, s32[6,6]{1,0:T(8,128)}, u32[]{:S(2)}) copy-start(s32[6,6]{1,0:T(8,128)} %cols_ref.1) | copy-start | bytes 436
  6.2 0.7 %copy-start.5 = (f32[256]{0:T(256)S(1)}, f32[256]{0:T(256)}, u32[]{:S(2)}) copy-start(f32[256]{0:T(256)} %param.12) | copy-start | bytes 3076

commit v2 on v1

v2 whole, which is shorter than its diff:
```python
import functools
import math

import jax
import jax.numpy as jnp
from jax import lax
from jax.experimental import pallas as pl
from jax.experimental.pallas import tpu as pltpu
from jax.sharding import PartitionSpec as P

MESH = pl.DeviceIdType.MESH
PLANE = 4
F32, BF16 = jnp.float32, jnp.bfloat16
NT = (((1,), (1,)), ((), ()))
TN = (((0,), (0,)), ((), ()))


def remote(src, dst, send_sem, recv_sem, device):
    return pltpu.make_async_remote_copy(
        src_ref=src, dst_ref=dst, send_sem=send_sem, recv_sem=recv_sem,
        device_id=device, device_id_type=MESH,
    )


def kernel(
    n, scale,
    cols_hbm, live_hbm, feat_hbm, tiles_hbm, w_hbm, b_hbm, cot_hbm,
    act_hbm, fg_hbm, wg_hbm, bg_hbm,
    act_ref, fg_ref, wg_ref, bg_ref, cols, live, w_ref, b_ref, feat, tiles, tiles_t, band, band_t, cot, eff, acc,
    p_send, p_recv, agg_all, grad_all, agg_grad, s_send, s_recv, t_send, t_recv,
    w_send, w_recv, z_recv, g_send, g_recv,
    local_sem, out_sem, f_ssem, f_rsem, p_ssem, p_rsem, s_ssem, s_rsem, t_ssem, t_rsem,
    w_ssem, w_rsem, z_ssem, z_rsem, g_ssem, g_rsem,
):
    me, rep = lax.axis_index("rows"), lax.axis_index("rep")
    nb, slots, tile = tiles_hbm.shape[0], tiles_hbm.shape[1], tiles_hbm.shape[2]
    rows = nb * tile
    width = w_hbm.shape[0]
    groups = n // PLANE
    quad = lax.rem(me, PLANE)
    layer = lax.div(me, PLANE)
    chunk = 2 * tile
    chunks = rows // chunk
    even = lax.rem(me, 2) == 0
    near = jnp.where(even, me + 1, me - 1)
    far = jnp.where(even, me - 1, me + 1)
    has_far = jnp.logical_and(far >= 0, far < n)
    partner = (me, 1 - rep)

    def plane_peer(d):
        return lax.rem(quad + d, PLANE)

    def layer_peer(d):
        return lax.rem(layer + d, groups)

    barrier = pltpu.get_barrier_semaphore()

    def greet(device):
        pl.semaphore_signal(barrier, inc=1, device_id=device, device_id_type=MESH)

    @pl.when(has_far)
    def _():
        greet((far, rep))

    greet((near, rep))
    greet(partner)
    for d in range(1, PLANE):
        greet((layer * PLANE + plane_peer(d), rep))
    for d in range(1, groups):
        greet((layer_peer(d) * PLANE + quad, rep))

    loads = [
        pltpu.make_async_copy(src, dst, local_sem.at[i])
        for i, (src, dst) in enumerate((
            (cols_hbm, cols), (live_hbm, live), (tiles_hbm, tiles.at[pl.ds(0, nb)]),
            (feat_hbm, feat.at[pl.ds(rows, rows)]), (w_hbm, w_ref), (b_hbm, b_ref),
            (cot_hbm, cot),
        ))
    ]
    for load in loads:
        load.start()

    pl.semaphore_wait(barrier, PLANE + groups + has_far.astype(jnp.int32))

    def far_feat(j):
        start = pl.multiple_of(jnp.where(even, j, chunks - 1 - j) * chunk, chunk)
        return remote(
            feat_hbm.at[pl.ds(start, chunk)], feat.at[pl.ds(j * chunk, chunk)],
            f_ssem.at[j], f_rsem.at[j], (far, rep),
        )

    near_feat = remote(
        feat_hbm, feat.at[pl.ds(2 * rows, rows)],
        f_ssem.at[chunks], f_rsem.at[chunks], (near, rep),
    )

    @pl.when(has_far)
    def _():
        for j in range(chunks):
            far_feat(j).start()

    near_feat.start()

    @pl.when(jnp.logical_not(has_far))
    def _():
        feat[:rows] = jnp.zeros((rows, width), BF16)
        s_recv[0] = jnp.zeros(s_recv.shape[1:], BF16)

    tiles[nb, 0] = jnp.zeros((tile, tile), BF16)
    tiles_t[nb, 0] = jnp.zeros((tile, tile), BF16)

    first = (me - 1) * nb
    loads[0].wait()
    loads[1].wait()
    for g in range(nb):
        count = live[0, g]
        for k in range(slots):
            block = cols[g, k] - first
            pair = lax.div(block, 2)
            turned = block + 2 * (nb // 2 - 1 - 2 * pair)
            from_even = jnp.where(block < nb, turned, block)
            from_odd = jnp.where(
                block < nb, block + 2 * nb, jnp.where(block < 2 * nb, block, block - 2 * nb)
            )
            eff[g * slots + k] = jnp.where(
                k < count, jnp.where(even, from_even, from_odd), -1
            )
    loads[2].wait()

    def slot_of(g, s):
        a, k_at = jnp.int32(nb), jnp.int32(0)
        for k in range(slots):
            hit = eff[g * slots + k] == s
            a = jnp.where(hit, g, a)
            k_at = jnp.where(hit, k, k_at)
        return a, k_at

    def place(s, carry):
        at = pl.ds(pl.multiple_of(s * tile, tile), tile)
        for g in range(nb):
            a, k_at = slot_of(g, s)
            band[g * tile:(g + 1) * tile, at] = tiles[a, k_at]
        return carry

    lax.fori_loop(0, 3 * nb, place, 0)

    def dot(a, b):
        return jnp.dot(a, b, preferred_element_type=F32)

    def chunk_at(m):
        return pl.ds(pl.multiple_of(m * chunk, chunk), chunk)

    loads[3].wait()
    near_feat.wait_recv()

    def near_rows(m, carry):
        acc[chunk_at(m), :] = dot(band[chunk_at(m), rows:], feat[rows:])
        return carry

    lax.fori_loop(0, chunks, near_rows, 0)

    def p_copy(j):
        return remote(p_send.at[j], p_recv.at[j], p_ssem.at[j], p_rsem.at[j], partner)

    def forward_chunk(j):
        return jnp.where(even, chunks - 1 - j, j)

    for j in range(chunks):
        @pl.when(has_far)
        def _():
            far_feat(j).wait_recv()

        at, reach = chunk_at(forward_chunk(j)), (j + 1) * chunk
        p_send[j] = (acc[at, :] + dot(band[at, :reach], feat[:reach])).astype(BF16)
        p_copy(j).start()

    def flip(g, carry):
        for k in range(slots):
            tiles_t[g, k] = tiles[g, k].T
        return carry

    lax.fori_loop(0, nb, flip, 0)

    def place_t(s, carry):
        at = pl.ds(pl.multiple_of(s * tile, tile), tile)
        for g in range(nb):
            a, k_at = slot_of(g, s)
            band_t[at, g * tile:(g + 1) * tile] = tiles_t[a, k_at]
        return carry

    lax.fori_loop(0, 3 * nb, place_t, 0)

    for load in loads[4:]:
        load.wait()
    for j in range(chunks):
        at = chunk_at(forward_chunk(j))
        p_copy(j).wait_recv()
        agg = (p_send[j].astype(F32) + p_recv[j].astype(F32)).astype(BF16)
        pre = dot(agg, w_ref[...]) + b_ref[...]
        sig = jax.nn.sigmoid(pre)
        pre_grad = (cot[at, :].astype(F32) * sig * (1.0 + pre * (1.0 - sig))).astype(BF16)
        agg_grad[at, :] = lax.dot_general(
            pre_grad, w_ref[...], NT, preferred_element_type=F32
        ).astype(BF16)
        act_ref[at, :] = (pre * sig).astype(BF16)
        agg_all[at, :] = agg
        grad_all[at, :] = pre_grad
    act_out = pltpu.make_async_copy(act_ref, act_hbm, out_sem.at[chunks])
    act_out.start()

    def far_copy(j):
        return remote(
            s_send.at[0, j], s_recv.at[0, j], s_ssem.at[j], s_rsem.at[j], (far, rep)
        )

    near_copy = remote(
        s_send.at[1], s_recv.at[1], s_ssem.at[chunks], s_rsem.at[chunks], (near, rep)
    )

    for j in range(chunks):
        s_send[0, j] = dot(band_t[j * chunk:(j + 1) * chunk, :], agg_grad[...]).astype(BF16)

        @pl.when(has_far)
        def _():
            far_copy(j).start()

    part = width // PLANE
    w_part = lax.dot_general(agg_all[...], grad_all[...], TN, preferred_element_type=F32)
    b_part = jnp.sum(grad_all[...].astype(F32), axis=0, keepdims=True)
    for c in range(PLANE):
        w_send[c, :part] = w_part[c * part:(c + 1) * part].astype(BF16)
        w_send[c, part:] = jnp.broadcast_to(b_part, (16, width)).astype(BF16)

    def w_copy(d, slot):
        peer = plane_peer(d)
        return remote(
            w_send.at[peer], w_recv.at[slot], w_ssem.at[d - 1], w_rsem.at[d - 1],
            (layer * PLANE + peer, rep),
        )

    for d in range(1, PLANE):
        w_copy(d, quad).start()
    w_recv[quad] = w_send[quad]

    def near_terms(m, carry):
        at = pl.ds(pl.multiple_of(2 * rows + m * chunk, chunk), chunk)
        s_send[1, m] = dot(band_t[at, :], agg_grad[...]).astype(BF16)
        return carry

    lax.fori_loop(0, chunks, near_terms, 0)
    near_copy.start()

    def own_terms(m, carry):
        at = pl.ds(pl.multiple_of(rows + m * chunk, chunk), chunk)
        acc[chunk_at(m), :] = dot(band_t[at, :], agg_grad[...])
        return carry

    lax.fori_loop(0, chunks, own_terms, 0)

    def t_copy(j):
        return remote(t_send.at[j], t_recv.at[j], t_ssem.at[j], t_rsem.at[j], partner)

    def z_copy(d, slot):
        return remote(
            z_recv.at[layer], z_recv.at[slot], z_ssem.at[d - 1], z_rsem.at[d - 1],
            (layer_peer(d) * PLANE + quad, rep),
        )

    def backward_chunk(j):
        return jnp.where(even, j, chunks - 1 - j)

    near_copy.wait_recv()
    for j in range(chunks):
        @pl.when(has_far)
        def _():
            far_copy(j).wait_recv()

        m = backward_chunk(j)
        t_send[j] = (
            acc[chunk_at(m), :] + s_recv[0, j].astype(F32) + s_recv[1, m].astype(F32)
        ).astype(BF16)
        t_copy(j).start()
        if j == 0:
            for d in range(1, PLANE):
                w_copy(d, lax.rem(quad + PLANE - d, PLANE)).wait_recv()
            z_recv[layer] = sum(w_recv[c].astype(F32) for c in range(PLANE)).astype(BF16)
            for d in range(1, groups):
                z_copy(d, layer).start()

    for d in range(1, groups):
        z_copy(d, lax.rem(layer + groups - d, groups)).wait_recv()
    total = sum(z_recv[c].astype(F32) for c in range(groups)) * scale
    bg_ref[...] = total[part:part + 1]
    bg_out = pltpu.make_async_copy(bg_ref, bg_hbm, out_sem.at[chunks + 1])
    bg_out.start()
    g_send[...] = total[:part].astype(BF16)
    g_recv[quad] = total[:part].astype(BF16)

    def g_copy(d, slot):
        return remote(
            g_send, g_recv.at[slot], g_ssem.at[d - 1], g_rsem.at[d - 1],
            (layer * PLANE + plane_peer(d), rep),
        )

    for d in range(1, PLANE):
        g_copy(d, quad).start()

    def fg_out(j):
        at = chunk_at(backward_chunk(j))
        return pltpu.make_async_copy(fg_ref.at[at], fg_hbm.at[at], out_sem.at[j])

    for j in range(chunks):
        t_copy(j).wait_recv()
        fg_ref[chunk_at(backward_chunk(j)), :] = (
            t_send[j].astype(F32) + t_recv[j].astype(F32)
        ).astype(BF16)
        fg_out(j).start()

    for d in range(1, PLANE):
        g_copy(d, lax.rem(quad + PLANE - d, PLANE)).wait_recv()
    for c in range(PLANE):
        wg_ref[c * part:(c + 1) * part, :] = g_recv[c].astype(F32)
    wg_out = pltpu.make_async_copy(wg_ref, wg_hbm, out_sem.at[chunks + 2])
    wg_out.start()

    @pl.when(has_far)
    def _():
        for j in range(chunks):
            far_feat(j).wait_send()
            far_copy(j).wait_send()

    near_feat.wait_send()
    near_copy.wait_send()
    for j in range(chunks):
        p_copy(j).wait_send()
        t_copy(j).wait_send()
    for d in range(1, PLANE):
        w_copy(d, quad).wait_send()
        g_copy(d, quad).wait_send()
    for d in range(1, groups):
        z_copy(d, layer).wait_send()

    for j in range(chunks):
        fg_out(j).wait()
    for out in (act_out, bg_out, wg_out):
        out.wait()


def hand_out(*refs):
    count = len(refs) // 2
    copies = [
        pltpu.make_async_copy(refs[i], refs[count + i], refs[-1].at[i]) for i in range(count)
    ]
    for copy in copies:
        copy.start()
    for copy in copies:
        copy.wait()


def solution(mesh):
    n = mesh.shape["rows"]

    def local(features, tiles, columns, live, weight, bias, cotangent):
        nb, slots, tile, _ = tiles.shape
        rows, width = features.shape
        chunk = 2 * tile
        chunks = rows // chunk
        groups = n // PLANE
        part = width // PLANE
        vmem, dma = pltpu.VMEM, pltpu.SemaphoreType.DMA
        hbm = pl.BlockSpec(memory_space=pltpu.HBM)
        shapes = (
            jax.ShapeDtypeStruct((rows, width), BF16),
            jax.ShapeDtypeStruct((rows, width), BF16),
            jax.ShapeDtypeStruct((width, width), F32),
            jax.ShapeDtypeStruct((1, width), F32),
        )
        results = pl.pallas_call(
            functools.partial(kernel, n, 1.0 / math.sqrt(rows * n)),
            out_shape=shapes,
            in_specs=[hbm] * 7,
            out_specs=(hbm,) * 4,
            scratch_shapes=[
                vmem((rows, width), BF16),
                vmem((rows, width), BF16),
                vmem((width, width), F32),
                vmem((1, width), F32),
                pltpu.SMEM((nb, slots), jnp.int32),
                pltpu.SMEM((1, nb), jnp.int32),
                vmem((width, width), BF16),
                vmem((1, width), F32),
                vmem((3 * rows, width), BF16),
                vmem((nb + 1, slots, tile, tile), BF16),
                vmem((nb + 1, slots, tile, tile), BF16),
                vmem((rows, 3 * rows), BF16),
                vmem((3 * rows, rows), BF16),
                vmem((rows, width), BF16),
                pltpu.SMEM((nb * slots,), jnp.int32),
                vmem((rows, width), F32),
                vmem((chunks, chunk, width), BF16),
                vmem((chunks, chunk, width), BF16),
                vmem((rows, width), BF16),
                vmem((rows, width), BF16),
                vmem((rows, width), BF16),
                vmem((2, chunks, chunk, width), BF16),
                vmem((2, chunks, chunk, width), BF16),
                vmem((chunks, chunk, width), BF16),
                vmem((chunks, chunk, width), BF16),
                vmem((PLANE, part + 16, width), BF16),
                vmem((PLANE, part + 16, width), BF16),
                vmem((groups, part + 16, width), BF16),
                vmem((part, width), BF16),
                vmem((PLANE, part, width), BF16),
                dma((7,)),
                dma((chunks + 3,)),
                dma((chunks + 1,)), dma((chunks + 1,)),
                dma((chunks,)), dma((chunks,)),
                dma((chunks + 1,)), dma((chunks + 1,)),
                dma((chunks,)), dma((chunks,)),
                dma((PLANE - 1,)), dma((PLANE - 1,)),
                dma((groups - 1,)), dma((groups - 1,)),
                dma((PLANE - 1,)), dma((PLANE - 1,)),
            ],
            compiler_params=pltpu.CompilerParams(
                collective_id=0, has_side_effects=True, vmem_limit_bytes=64 * 2**20
            ),
        )(columns, live.T, features, tiles, weight, bias.reshape(1, width), cotangent)
        act, feature_grad, weight_grad, bias_grad = pl.pallas_call(
            hand_out,
            out_shape=shapes,
            in_specs=[hbm] * 4,
            out_specs=(hbm,) * 4,
            scratch_shapes=[dma((4,))],
            compiler_params=pltpu.CompilerParams(vmem_limit_bytes=64 * 2**20),
        )(*results)
        return act, feature_grad, weight_grad, bias_grad.reshape(width)

    return jax.shard_map(
        local,
        mesh=mesh,
        in_specs=(
            P("rows", None), P("rows", "rep", None, None), P("rows", "rep"), P("rows", "rep"),
            P(), P(), P("rows", None),
        ),
        out_specs=(P("rows", None), P("rows", None), P(), P()),
        check_vma=False,
    )
```

time: 49.8 us -> 72.7 us (1.46)
  Pallas kernels: 39.3 us -> 71.9 us
  local copies, waits for them, and re-layouts: 9.03 us -> 0 us
    pallas_call x0 -> x1, Pallas kernels: none -> 32.9 us  [local(): pl.pallas_call(hand_out, out_shape=shapes, in_specs=[hbm] * 4, out_specs=...]
    unnamed x17 -> x0, local copies, waits for them, and re-layouts: 9.03 us -> none
where the time goes in v2:
time: 72.7 us; the launch traced here: 72.5 us
  Pallas kernels  71.9 us (99%)
    pallas_call x1, Pallas kernels, local(): pl.pallas_call(functools.partial(kernel, n, 1.0 / math.sqrt(rows * n)), o...  39 us
    pallas_call x1, Pallas kernels, local(): pl.pallas_call(hand_out, out_shape=shapes, in_specs=[hbm] * 4, out_specs=...  32.9 us

profile of v2, /device:TPU:0, one launch (start us, length us, event | category | flops | bytes accessed | tf_op | source)
XLA Modules:
  0.0 72.5 jit_solution(1585029489858336942)
XLA Ops:
  0.6 39.0 %shard_map.102 = (bf16[768,256]{1,0:T(8,128)(2,1)}, bf16[768,256]{1,0:T(8,128)(2,1)}, f32[256,256]{1,0:T(8,128)}, f32[1,256]{1,0:T(1,128)}) custom-call(s32[6,6]{1,0:T(8,128)} %cols_hbm.1, s32[1,6]{1,0:T(1,128)} %bitcast.4, bf16[768,256]{1,0:T(8,128)(2,1)} %feat_hbm.1, bf16[6,6,128,128]{3,2,1,0:T(8,128)(2,1)} %tiles_hbm.1, bf16[256,256]{1,0:T(8,128)(2,1)} %w_hbm.1, ...), custom_call_target="tpu_custom_call" | custom-call | tf_op jit(solution)/shard_map/pallas_call | solution.py:378
  39.6 32.9 %shard_map.103 = (bf16[768,256]{1,0:T(8,128)(2,1)}, bf16[768,256]{1,0:T(8,128)(2,1)}, f32[256,256]{1,0:T(8,128)}, f32[1,256]{1,0:T(1,128)}) custom-call(bf16[768,256]{1,0:T(8,128)(2,1)} %get-tuple-element.12.refs_0_, bf16[768,256]{1,0:T(8,128)(2,1)} %get-tuple-element.13.refs_1_, f32[256,256]{1,0:T(8,128)} %get-tuple-element.14.refs_2_, ...), custom_call_target="tpu_custom_call" | custom-call | tf_op jit(solution)/shard_map/pallas_call | solution.py:428

commit v3 on v2

--- a/solution.py
+++ b/solution.py
@@ -39,12 +39,14 @@
     groups = n // PLANE
     quad = lax.rem(me, PLANE)
     layer = lax.div(me, PLANE)
-    chunk = 2 * tile
-    chunks = rows // chunk
+    chunk, chunks = tile, nb
+    bulk = 2 * tile
     even = lax.rem(me, 2) == 0
     near = jnp.where(even, me + 1, me - 1)
     far = jnp.where(even, me - 1, me + 1)
     has_far = jnp.logical_and(far >= 0, far < n)
+    far_even = jnp.logical_and(has_far, even)
+    far_odd = jnp.logical_and(has_far, jnp.logical_not(even))
     partner = (me, 1 - rep)
 
     def plane_peer(d):
@@ -66,6 +68,7 @@
     greet(partner)
     for d in range(1, PLANE):
         greet((layer * PLANE + plane_peer(d), rep))
+        greet((layer * PLANE + plane_peer(d), 1 - rep))
     for d in range(1, groups):
         greet((layer_peer(d) * PLANE + quad, rep))
 
@@ -80,31 +83,41 @@
     for load in loads:
         load.start()
 
-    pl.semaphore_wait(barrier, PLANE + groups + has_far.astype(jnp.int32))
+    loads[3].wait()
+    pl.semaphore_wait(barrier, 2 * PLANE - 1 + groups + has_far.astype(jnp.int32))
 
     def far_feat(j):
         start = pl.multiple_of(jnp.where(even, j, chunks - 1 - j) * chunk, chunk)
         return remote(
-            feat_hbm.at[pl.ds(start, chunk)], feat.at[pl.ds(j * chunk, chunk)],
+            feat.at[pl.ds(rows + start, chunk)], feat.at[pl.ds(j * chunk, chunk)],
             f_ssem.at[j], f_rsem.at[j], (far, rep),
         )
 
     near_feat = remote(
-        feat_hbm, feat.at[pl.ds(2 * rows, rows)],
+        feat.at[pl.ds(rows, rows)], feat.at[pl.ds(2 * rows, rows)],
         f_ssem.at[chunks], f_rsem.at[chunks], (near, rep),
     )
 
-    @pl.when(has_far)
-    def _():
-        for j in range(chunks):
+    for j in range(chunks):
+        @pl.when(has_far if j < chunks - 1 else far_odd)
+        def _():
             far_feat(j).start()
 
     near_feat.start()
+    last = (chunks - 1) * chunk
 
     @pl.when(jnp.logical_not(has_far))
     def _():
-        feat[:rows] = jnp.zeros((rows, width), BF16)
-        s_recv[0] = jnp.zeros(s_recv.shape[1:], BF16)
+        feat[:last] = jnp.zeros((last, width), BF16)
+        s_recv[0, :last] = jnp.zeros((last, width), BF16)
+
+    @pl.when(jnp.logical_not(far_even))
+    def _():
+        feat[last:rows] = jnp.zeros((chunk, width), BF16)
+
+    @pl.when(jnp.logical_not(far_odd))
+    def _():
+        s_recv[0, last:] = jnp.zeros((chunk, width), BF16)
 
     tiles[nb, 0] = jnp.zeros((tile, tile), BF16)
     tiles_t[nb, 0] = jnp.zeros((tile, tile), BF16)
@@ -116,9 +129,7 @@
         count = live[0, g]
         for k in range(slots):
             block = cols[g, k] - first
-            pair = lax.div(block, 2)
-            turned = block + 2 * (nb // 2 - 1 - 2 * pair)
-            from_even = jnp.where(block < nb, turned, block)
+            from_even = jnp.where(block < nb, nb - 1 - block, block)
             from_odd = jnp.where(
                 block < nb, block + 2 * nb, jnp.where(block < 2 * nb, block, block - 2 * nb)
             )
@@ -150,36 +161,27 @@
     def chunk_at(m):
         return pl.ds(pl.multiple_of(m * chunk, chunk), chunk)
 
-    loads[3].wait()
+    def bulk_at(m):
+        return pl.ds(pl.multiple_of(m * bulk, bulk), bulk)
+
     near_feat.wait_recv()
 
     def near_rows(m, carry):
-        acc[chunk_at(m), :] = dot(band[chunk_at(m), rows:], feat[rows:])
-        return carry
-
-    lax.fori_loop(0, chunks, near_rows, 0)
+        acc[bulk_at(m), :] = dot(band[bulk_at(m), rows:], feat[rows:])
+        return carry
+
+    lax.fori_loop(0, rows // bulk, near_rows, 0)
 
     def p_copy(j):
         return remote(p_send.at[j], p_recv.at[j], p_ssem.at[j], p_rsem.at[j], partner)
 
     def forward_chunk(j):
         return jnp.where(even, chunks - 1 - j, j)
-
-    for j in range(chunks):
-        @pl.when(has_far)
-        def _():
-            far_feat(j).wait_recv()
-
-        at, reach = chunk_at(forward_chunk(j)), (j + 1) * chunk
-        p_send[j] = (acc[at, :] + dot(band[at, :reach], feat[:reach])).astype(BF16)
-        p_copy(j).start()
 
     def flip(g, carry):
         for k in range(slots):
             tiles_t[g, k] = tiles[g, k].T
         return carry
-
-    lax.fori_loop(0, nb, flip, 0)
 
     def place_t(s, carry):
         at = pl.ds(pl.multiple_of(s * tile, tile), tile)
@@ -188,7 +190,18 @@
             band_t[at, g * tile:(g + 1) * tile] = tiles_t[a, k_at]
         return carry
 
-    lax.fori_loop(0, 3 * nb, place_t, 0)
+    for j in range(chunks):
+        @pl.when(has_far if j < chunks - 1 else far_even)
+        def _():
+            far_feat(j).wait_recv()
+
+        at, reach = chunk_at(forward_chunk(j)), (j + 1) * chunk
+        p_send[j] = (acc[at, :] + dot(band[at, :reach], feat[:reach])).astype(BF16)
+        p_copy(j).start()
+        if j < 3:
+            lax.fori_loop(j * nb // 3, (j + 1) * nb // 3, flip, 0)
+        elif j < 5:
+            lax.fori_loop(6 * nb // 4 * (j - 3), 6 * nb // 4 * (j - 2), place_t, 0)
 
     for load in loads[4:]:
         load.wait()
@@ -209,23 +222,30 @@
     act_out.start()
 
     def far_copy(j):
+        piece = pl.ds(j * chunk, chunk)
         return remote(
-            s_send.at[0, j], s_recv.at[0, j], s_ssem.at[j], s_rsem.at[j], (far, rep)
+            s_send.at[0, piece], s_recv.at[0, piece], s_ssem.at[j], s_rsem.at[j], (far, rep)
         )
 
     near_copy = remote(
         s_send.at[1], s_recv.at[1], s_ssem.at[chunks], s_rsem.at[chunks], (near, rep)
     )
 
-    for j in range(chunks):
-        s_send[0, j] = dot(band_t[j * chunk:(j + 1) * chunk, :], agg_grad[...]).astype(BF16)
-
-        @pl.when(has_far)
+    def far_terms(j):
+        at = slice(j * chunk, (j + 1) * chunk)
+        s_send[0, at] = dot(band_t[at, :], agg_grad[...]).astype(BF16)
+
+        @pl.when(has_far if j < chunks - 1 else far_even)
         def _():
             far_copy(j).start()
 
-    part = width // PLANE
-    w_part = lax.dot_general(agg_all[...], grad_all[...], TN, preferred_element_type=F32)
+    for j in range(chunks // 2):
+        far_terms(j)
+
+    half = width // 2
+    part = half // PLANE
+    mine = pl.ds(pl.multiple_of(rep * half, half), half)
+    w_part = lax.dot_general(agg_all[:, mine], grad_all[...], TN, preferred_element_type=F32)
     b_part = jnp.sum(grad_all[...].astype(F32), axis=0, keepdims=True)
     for c in range(PLANE):
         w_send[c, :part] = w_part[c * part:(c + 1) * part].astype(BF16)
@@ -242,20 +262,23 @@
         w_copy(d, quad).start()
     w_recv[quad] = w_send[quad]
 
+    for j in range(chunks // 2, chunks):
+        far_terms(j)
+
     def near_terms(m, carry):
-        at = pl.ds(pl.multiple_of(2 * rows + m * chunk, chunk), chunk)
-        s_send[1, m] = dot(band_t[at, :], agg_grad[...]).astype(BF16)
-        return carry
-
-    lax.fori_loop(0, chunks, near_terms, 0)
+        at = pl.ds(pl.multiple_of(2 * rows + m * bulk, bulk), bulk)
+        s_send[1, bulk_at(m)] = dot(band_t[at, :], agg_grad[...]).astype(BF16)
+        return carry
+
+    lax.fori_loop(0, rows // bulk, near_terms, 0)
     near_copy.start()
 
     def own_terms(m, carry):
-        at = pl.ds(pl.multiple_of(rows + m * chunk, chunk), chunk)
-        acc[chunk_at(m), :] = dot(band_t[at, :], agg_grad[...])
-        return carry
-
-    lax.fori_loop(0, chunks, own_terms, 0)
+        at = pl.ds(pl.multiple_of(rows + m * bulk, bulk), bulk)
+        acc[bulk_at(m), :] = dot(band_t[at, :], agg_grad[...])
+        return carry
+
+    lax.fori_loop(0, rows // bulk, own_terms, 0)
 
     def t_copy(j):
         return remote(t_send.at[j], t_recv.at[j], t_ssem.at[j], t_rsem.at[j], partner)
@@ -271,16 +294,17 @@
 
     near_copy.wait_recv()
     for j in range(chunks):
-        @pl.when(has_far)
+        @pl.when(has_far if j < chunks - 1 else far_odd)
         def _():
             far_copy(j).wait_recv()
 
-        m = backward_chunk(j)
+        at = chunk_at(backward_chunk(j))
         t_send[j] = (
-            acc[chunk_at(m), :] + s_recv[0, j].astype(F32) + s_recv[1, m].astype(F32)
+            acc[at, :] + s_recv[0, j * chunk:(j + 1) * chunk].astype(F32)
+            + s_recv[1, at].astype(F32)
         ).astype(BF16)
         t_copy(j).start()
-        if j == 0:
+        if j == 1:
             for d in range(1, PLANE):
                 w_copy(d, lax.rem(quad + PLANE - d, PLANE)).wait_recv()
             z_recv[layer] = sum(w_recv[c].astype(F32) for c in range(PLANE)).astype(BF16)
@@ -294,16 +318,18 @@
     bg_out = pltpu.make_async_copy(bg_ref, bg_hbm, out_sem.at[chunks + 1])
     bg_out.start()
     g_send[...] = total[:part].astype(BF16)
-    g_recv[quad] = total[:part].astype(BF16)
-
-    def g_copy(d, slot):
+    g_recv[rep * PLANE + quad] = total[:part].astype(BF16)
+
+    def g_copy(turn, d, slot):
+        at = turn * PLANE + d - 1
         return remote(
-            g_send, g_recv.at[slot], g_ssem.at[d - 1], g_rsem.at[d - 1],
-            (layer * PLANE + plane_peer(d), rep),
-        )
-
-    for d in range(1, PLANE):
-        g_copy(d, quad).start()
+            g_send, g_recv.at[slot], g_ssem.at[at], g_rsem.at[at],
+            (layer * PLANE + plane_peer(d), 1 - rep if turn else rep),
+        )
+
+    others = [(turn, d) for turn in range(2) for d in range(PLANE) if turn or d]
+    for turn, d in others:
+        g_copy(turn, d, rep * PLANE + quad).start()
 
     def fg_out(j):
         at = chunk_at(backward_chunk(j))
@@ -316,17 +342,21 @@
         ).astype(BF16)
         fg_out(j).start()
 
-    for d in range(1, PLANE):
-        g_copy(d, lax.rem(quad + PLANE - d, PLANE)).wait_recv()
-    for c in range(PLANE):
+    for turn, d in others:
+        source = lax.rem(quad + PLANE - d, PLANE)
+        g_copy(turn, d, (1 - rep if turn else rep) * PLANE + source).wait_recv()
+    for c in range(2 * PLANE):
         wg_ref[c * part:(c + 1) * part, :] = g_recv[c].astype(F32)
     wg_out = pltpu.make_async_copy(wg_ref, wg_hbm, out_sem.at[chunks + 2])
     wg_out.start()
 
-    @pl.when(has_far)
-    def _():
-        for j in range(chunks):
+    for j in range(chunks):
+        @pl.when(has_far if j < chunks - 1 else far_odd)
+        def _():
             far_feat(j).wait_send()
+
+        @pl.when(has_far if j < chunks - 1 else far_even)
+        def _():
             far_copy(j).wait_send()
 
     near_feat.wait_send()
@@ -336,7 +366,8 @@
         t_copy(j).wait_send()
     for d in range(1, PLANE):
         w_copy(d, quad).wait_send()
-        g_copy(d, quad).wait_send()
+    for turn, d in others:
+        g_copy(turn, d, rep * PLANE + quad).wait_send()
     for d in range(1, groups):
         z_copy(d, layer).wait_send()
 
@@ -347,14 +378,17 @@
 
 
 def hand_out(*refs):
-    count = len(refs) // 2
-    copies = [
-        pltpu.make_async_copy(refs[i], refs[count + i], refs[-1].at[i]) for i in range(count)
-    ]
-    for copy in copies:
-        copy.start()
-    for copy in copies:
-        copy.wait()
+    sources, results, held = refs[:4], refs[4:8], refs[8:12]
+    sem = refs[12]
+    loads = [pltpu.make_async_copy(sources[i], held[i], sem.at[0, i]) for i in range(4)]
+    stores = [pltpu.make_async_copy(held[i], results[i], sem.at[1, i]) for i in range(4)]
+    for load in loads:
+        load.start()
+    for load, store in zip(loads, stores):
+        load.wait()
+        store.start()
+    for store in stores:
+        store.wait()
 
 
 def solution(mesh):
@@ -363,10 +397,9 @@
     def local(features, tiles, columns, live, weight, bias, cotangent):
         nb, slots, tile, _ = tiles.shape
         rows, width = features.shape
-        chunk = 2 * tile
-        chunks = rows // chunk
+        chunk, chunks = tile, nb
         groups = n // PLANE
-        part = width // PLANE
+        part = width // (2 * PLANE)
         vmem, dma = pltpu.VMEM, pltpu.SemaphoreType.DMA
         hbm = pl.BlockSpec(memory_space=pltpu.HBM)
         shapes = (
@@ -402,15 +435,15 @@
                 vmem((rows, width), BF16),
                 vmem((rows, width), BF16),
                 vmem((rows, width), BF16),
-                vmem((2, chunks, chunk, width), BF16),
-                vmem((2, chunks, chunk, width), BF16),
+                vmem((2, rows, width), BF16),
+                vmem((2, rows, width), BF16),
                 vmem((chunks, chunk, width), BF16),
                 vmem((chunks, chunk, width), BF16),
                 vmem((PLANE, part + 16, width), BF16),
                 vmem((PLANE, part + 16, width), BF16),
                 vmem((groups, part + 16, width), BF16),
                 vmem((part, width), BF16),
-                vmem((PLANE, part, width), BF16),
+                vmem((2 * PLANE, part, width), BF16),
                 dma((7,)),
                 dma((chunks + 3,)),
                 dma((chunks + 1,)), dma((chunks + 1,)),
@@ -419,7 +452,7 @@
                 dma((chunks,)), dma((chunks,)),
                 dma((PLANE - 1,)), dma((PLANE - 1,)),
                 dma((groups - 1,)), dma((groups - 1,)),
-                dma((PLANE - 1,)), dma((PLANE - 1,)),
+                dma((2 * PLANE - 1,)), dma((2 * PLANE - 1,)),
             ],
             compiler_params=pltpu.CompilerParams(
                 collective_id=0, has_side_effects=True, vmem_limit_bytes=64 * 2**20
@@ -430,7 +463,7 @@
             out_shape=shapes,
             in_specs=[hbm] * 4,
             out_specs=(hbm,) * 4,
-            scratch_shapes=[dma((4,))],
+            scratch_shapes=[vmem(x.shape, x.dtype) for x in shapes] + [dma((2, 4))],
             compiler_params=pltpu.CompilerParams(vmem_limit_bytes=64 * 2**20),
         )(*results)
         return act, feature_grad, weight_grad, bias_grad.reshape(width)

time: 72.7 us -> 39.7 us (0.55)
  Pallas kernels: 71.9 us -> 38.9 us
    pallas_call x1, Pallas kernels: 32.9 us -> 2.03 us  [local(): pl.pallas_call(hand_out, out_shape=shapes, in_specs=[hbm] * 4, out_specs=...]
    pallas_call x1, Pallas kernels: 39 us -> 36.9 us  [local(): pl.pallas_call(functools.partial(kernel, n, 1.0 / math.sqrt(rows * n)), o...]
where the time goes in v3:
time: 39.7 us; the launch traced here: 39.5 us
  Pallas kernels  38.9 us (98%)
  between operations  0.64 us (2%)
    pallas_call x1, Pallas kernels, local(): pl.pallas_call(functools.partial(kernel, n, 1.0 / math.sqrt(rows * n)), o...  36.9 us
    pallas_call x1, Pallas kernels, local(): pl.pallas_call(hand_out, out_shape=shapes, in_specs=[hbm] * 4, out_specs=...  2.03 us

profile of v3, /device:TPU:0, one launch (start us, length us, event | category | flops | bytes accessed | tf_op | source)
XLA Modules:
  0.0 39.5 jit_solution(2156733499251842127)
XLA Ops:
  0.6 36.9 %shard_map.102 = (bf16[768,256]{1,0:T(8,128)(2,1)}, bf16[768,256]{1,0:T(8,128)(2,1)}, f32[256,256]{1,0:T(8,128)}, f32[1,256]{1,0:T(1,128)}) custom-call(s32[6,6]{1,0:T(8,128)} %cols_hbm.1, s32[1,6]{1,0:T(1,128)} %bitcast.4, bf16[768,256]{1,0:T(8,128)(2,1)} %feat_hbm.1, bf16[6,6,128,128]{3,2,1,0:T(8,128)(2,1)} %tiles_hbm.1, bf16[256,256]{1,0:T(8,128)(2,1)} %w_hbm.1, ...), custom_call_target="tpu_custom_call" | custom-call | tf_op jit(solution)/shard_map/pallas_call | solution.py:411
  37.5 2.0 %shard_map.103 = (bf16[768,256]{1,0:T(8,128)(2,1)}, bf16[768,256]{1,0:T(8,128)(2,1)}, f32[256,256]{1,0:T(8,128)}, f32[1,256]{1,0:T(1,128)}) custom-call(bf16[768,256]{1,0:T(8,128)(2,1)} %get-tuple-element.12.refs_0_, bf16[768,256]{1,0:T(8,128)(2,1)} %get-tuple-element.13.refs_1_, f32[256,256]{1,0:T(8,128)} %get-tuple-element.14.refs_2_, ...), custom_call_target="tpu_custom_call" | custom-call | tf_op jit(solution)/shard_map/pallas_call | solution.py:461

commit v4 on v3

--- a/solution.py
+++ b/solution.py
@@ -26,8 +26,8 @@
     n, scale,
     cols_hbm, live_hbm, feat_hbm, tiles_hbm, w_hbm, b_hbm, cot_hbm,
     act_hbm, fg_hbm, wg_hbm, bg_hbm,
-    act_ref, fg_ref, wg_ref, bg_ref, cols, live, w_ref, b_ref, feat, tiles, tiles_t, band, band_t, cot, eff, acc,
-    p_send, p_recv, agg_all, grad_all, agg_grad, s_send, s_recv, t_send, t_recv,
+    act_ref, fg_ref, wg_ref, bg_ref, cols, live, w_ref, b_ref, feat, tiles, band, cot, eff, acc, acc_t,
+    p_send, p_recv, agg_all, grad_all, agg_grad_t, s_send, s_recv, t_send, t_recv,
     w_send, w_recv, z_recv, g_send, g_recv,
     local_sem, out_sem, f_ssem, f_rsem, p_ssem, p_rsem, s_ssem, s_rsem, t_ssem, t_rsem,
     w_ssem, w_rsem, z_ssem, z_rsem, g_ssem, g_rsem,
@@ -83,45 +83,6 @@
     for load in loads:
         load.start()
 
-    loads[3].wait()
-    pl.semaphore_wait(barrier, 2 * PLANE - 1 + groups + has_far.astype(jnp.int32))
-
-    def far_feat(j):
-        start = pl.multiple_of(jnp.where(even, j, chunks - 1 - j) * chunk, chunk)
-        return remote(
-            feat.at[pl.ds(rows + start, chunk)], feat.at[pl.ds(j * chunk, chunk)],
-            f_ssem.at[j], f_rsem.at[j], (far, rep),
-        )
-
-    near_feat = remote(
-        feat.at[pl.ds(rows, rows)], feat.at[pl.ds(2 * rows, rows)],
-        f_ssem.at[chunks], f_rsem.at[chunks], (near, rep),
-    )
-
-    for j in range(chunks):
-        @pl.when(has_far if j < chunks - 1 else far_odd)
-        def _():
-            far_feat(j).start()
-
-    near_feat.start()
-    last = (chunks - 1) * chunk
-
-    @pl.when(jnp.logical_not(has_far))
-    def _():
-        feat[:last] = jnp.zeros((last, width), BF16)
-        s_recv[0, :last] = jnp.zeros((last, width), BF16)
-
-    @pl.when(jnp.logical_not(far_even))
-    def _():
-        feat[last:rows] = jnp.zeros((chunk, width), BF16)
-
-    @pl.when(jnp.logical_not(far_odd))
-    def _():
-        s_recv[0, last:] = jnp.zeros((chunk, width), BF16)
-
-    tiles[nb, 0] = jnp.zeros((tile, tile), BF16)
-    tiles_t[nb, 0] = jnp.zeros((tile, tile), BF16)
-
     first = (me - 1) * nb
     loads[0].wait()
     loads[1].wait()
@@ -136,6 +97,44 @@
             eff[g * slots + k] = jnp.where(
                 k < count, jnp.where(even, from_even, from_odd), -1
             )
+    loads[3].wait()
+    pl.semaphore_wait(barrier, 2 * PLANE - 1 + groups + has_far.astype(jnp.int32))
+
+    def far_feat(j):
+        start = pl.multiple_of(jnp.where(even, j, chunks - 1 - j) * chunk, chunk)
+        return remote(
+            feat.at[pl.ds(rows + start, chunk)], feat.at[pl.ds(j * chunk, chunk)],
+            f_ssem.at[j], f_rsem.at[j], (far, rep),
+        )
+
+    near_feat = remote(
+        feat.at[pl.ds(rows, rows)], feat.at[pl.ds(2 * rows, rows)],
+        f_ssem.at[chunks], f_rsem.at[chunks], (near, rep),
+    )
+
+    for j in range(chunks):
+        @pl.when(has_far if j < chunks - 1 else far_odd)
+        def _():
+            far_feat(j).start()
+
+    near_feat.start()
+    last = (chunks - 1) * chunk
+
+    @pl.when(jnp.logical_not(has_far))
+    def _():
+        feat[:last] = jnp.zeros((last, width), BF16)
+        s_recv[0, :chunks - 1] = jnp.zeros((chunks - 1, width, chunk), BF16)
+
+    @pl.when(jnp.logical_not(far_even))
+    def _():
+        feat[last:rows] = jnp.zeros((chunk, width), BF16)
+
+    @pl.when(jnp.logical_not(far_odd))
+    def _():
+        s_recv[0, chunks - 1] = jnp.zeros((width, chunk), BF16)
+
+    tiles[nb, 0] = jnp.zeros((tile, tile), BF16)
+
     loads[2].wait()
 
     def slot_of(g, s):
@@ -178,18 +177,6 @@
     def forward_chunk(j):
         return jnp.where(even, chunks - 1 - j, j)
 
-    def flip(g, carry):
-        for k in range(slots):
-            tiles_t[g, k] = tiles[g, k].T
-        return carry
-
-    def place_t(s, carry):
-        at = pl.ds(pl.multiple_of(s * tile, tile), tile)
-        for g in range(nb):
-            a, k_at = slot_of(g, s)
-            band_t[at, g * tile:(g + 1) * tile] = tiles_t[a, k_at]
-        return carry
-
     for j in range(chunks):
         @pl.when(has_far if j < chunks - 1 else far_even)
         def _():
@@ -198,10 +185,6 @@
         at, reach = chunk_at(forward_chunk(j)), (j + 1) * chunk
         p_send[j] = (acc[at, :] + dot(band[at, :reach], feat[:reach])).astype(BF16)
         p_copy(j).start()
-        if j < 3:
-            lax.fori_loop(j * nb // 3, (j + 1) * nb // 3, flip, 0)
-        elif j < 5:
-            lax.fori_loop(6 * nb // 4 * (j - 3), 6 * nb // 4 * (j - 2), place_t, 0)
 
     for load in loads[4:]:
         load.wait()
@@ -212,8 +195,8 @@
         pre = dot(agg, w_ref[...]) + b_ref[...]
         sig = jax.nn.sigmoid(pre)
         pre_grad = (cot[at, :].astype(F32) * sig * (1.0 + pre * (1.0 - sig))).astype(BF16)
-        agg_grad[at, :] = lax.dot_general(
-            pre_grad, w_ref[...], NT, preferred_element_type=F32
+        agg_grad_t[:, at] = lax.dot_general(
+            w_ref[...], pre_grad, NT, preferred_element_type=F32
         ).astype(BF16)
         act_ref[at, :] = (pre * sig).astype(BF16)
         agg_all[at, :] = agg
@@ -222,9 +205,8 @@
     act_out.start()
 
     def far_copy(j):
-        piece = pl.ds(j * chunk, chunk)
         return remote(
-            s_send.at[0, piece], s_recv.at[0, piece], s_ssem.at[j], s_rsem.at[j], (far, rep)
+            s_send.at[0, j], s_recv.at[0, j], s_ssem.at[j], s_rsem.at[j], (far, rep)
         )
 
     near_copy = remote(
@@ -233,7 +215,7 @@
 
     def far_terms(j):
         at = slice(j * chunk, (j + 1) * chunk)
-        s_send[0, at] = dot(band_t[at, :], agg_grad[...]).astype(BF16)
+        s_send[0, j] = dot(agg_grad_t[...], band[:, at]).astype(BF16)
 
         @pl.when(has_far if j < chunks - 1 else far_even)
         def _():
@@ -265,20 +247,18 @@
     for j in range(chunks // 2, chunks):
         far_terms(j)
 
-    def near_terms(m, carry):
-        at = pl.ds(pl.multiple_of(2 * rows + m * bulk, bulk), bulk)
-        s_send[1, bulk_at(m)] = dot(band_t[at, :], agg_grad[...]).astype(BF16)
-        return carry
-
-    lax.fori_loop(0, rows // bulk, near_terms, 0)
+    for j in range(0, chunks, 2):
+        at = slice(2 * rows + j * chunk, 2 * rows + (j + 2) * chunk)
+        terms = dot(agg_grad_t[...], band[:, at]).astype(BF16)
+        s_send[1, j] = terms[:, :chunk]
+        s_send[1, j + 1] = terms[:, chunk:]
     near_copy.start()
 
-    def own_terms(m, carry):
-        at = pl.ds(pl.multiple_of(rows + m * bulk, bulk), bulk)
-        acc[bulk_at(m), :] = dot(band_t[at, :], agg_grad[...])
-        return carry
-
-    lax.fori_loop(0, rows // bulk, own_terms, 0)
+    for j in range(0, chunks, 2):
+        at = slice(rows + j * chunk, rows + (j + 2) * chunk)
+        terms = dot(agg_grad_t[...], band[:, at])
+        acc_t[j] = terms[:, :chunk]
+        acc_t[j + 1] = terms[:, chunk:]
 
     def t_copy(j):
         return remote(t_send.at[j], t_recv.at[j], t_ssem.at[j], t_rsem.at[j], partner)
@@ -292,16 +272,38 @@
     def backward_chunk(j):
         return jnp.where(even, j, chunks - 1 - j)
 
+    def g_copy(turn, d, slot):
+        at = turn * PLANE + d - 1
+        return remote(
+            g_send, g_recv.at[slot], g_ssem.at[at], g_rsem.at[at],
+            (layer * PLANE + plane_peer(d), 1 - rep if turn else rep),
+        )
+
+    others = [(turn, d) for turn in range(2) for d in range(PLANE) if turn or d]
+
+    bg_out = pltpu.make_async_copy(bg_ref, bg_hbm, out_sem.at[chunks + 1])
+
+    def finish_weight():
+        for d in range(1, groups):
+            z_copy(d, lax.rem(layer + groups - d, groups)).wait_recv()
+        total = sum(z_recv[c].astype(F32) for c in range(groups)) * scale
+        bg_ref[...] = total[part:part + 1]
+        bg_out.start()
+        g_send[...] = total[:part].astype(BF16)
+        g_recv[rep * PLANE + quad] = total[:part].astype(BF16)
+
+        for turn, d in others:
+            g_copy(turn, d, rep * PLANE + quad).start()
+
     near_copy.wait_recv()
     for j in range(chunks):
         @pl.when(has_far if j < chunks - 1 else far_odd)
         def _():
             far_copy(j).wait_recv()
 
-        at = chunk_at(backward_chunk(j))
+        m = backward_chunk(j)
         t_send[j] = (
-            acc[at, :] + s_recv[0, j * chunk:(j + 1) * chunk].astype(F32)
-            + s_recv[1, at].astype(F32)
+            acc_t[m] + s_recv[0, j].astype(F32) + s_recv[1, m].astype(F32)
         ).astype(BF16)
         t_copy(j).start()
         if j == 1:
@@ -310,26 +312,8 @@
             z_recv[layer] = sum(w_recv[c].astype(F32) for c in range(PLANE)).astype(BF16)
             for d in range(1, groups):
                 z_copy(d, layer).start()
-
-    for d in range(1, groups):
-        z_copy(d, lax.rem(layer + groups - d, groups)).wait_recv()
-    total = sum(z_recv[c].astype(F32) for c in range(groups)) * scale
-    bg_ref[...] = total[part:part + 1]
-    bg_out = pltpu.make_async_copy(bg_ref, bg_hbm, out_sem.at[chunks + 1])
-    bg_out.start()
-    g_send[...] = total[:part].astype(BF16)
-    g_recv[rep * PLANE + quad] = total[:part].astype(BF16)
-
-    def g_copy(turn, d, slot):
-        at = turn * PLANE + d - 1
-        return remote(
-            g_send, g_recv.at[slot], g_ssem.at[at], g_rsem.at[at],
-            (layer * PLANE + plane_peer(d), 1 - rep if turn else rep),
-        )
-
-    others = [(turn, d) for turn in range(2) for d in range(PLANE) if turn or d]
-    for turn, d in others:
-        g_copy(turn, d, rep * PLANE + quad).start()
+        if j == chunks - 2:
+            finish_weight()
 
     def fg_out(j):
         at = chunk_at(backward_chunk(j))
@@ -339,7 +323,7 @@
         t_copy(j).wait_recv()
         fg_ref[chunk_at(backward_chunk(j)), :] = (
             t_send[j].astype(F32) + t_recv[j].astype(F32)
-        ).astype(BF16)
+        ).T.astype(BF16)
         fg_out(j).start()
 
     for turn, d in others:
@@ -424,21 +408,20 @@
                 vmem((1, width), F32),
                 vmem((3 * rows, width), BF16),
                 vmem((nb + 1, slots, tile, tile), BF16),
-                vmem((nb + 1, slots, tile, tile), BF16),
                 vmem((rows, 3 * rows), BF16),
-                vmem((3 * rows, rows), BF16),
                 vmem((rows, width), BF16),
                 pltpu.SMEM((nb * slots,), jnp.int32),
                 vmem((rows, width), F32),
+                vmem((chunks, width, chunk), F32),
                 vmem((chunks, chunk, width), BF16),
                 vmem((chunks, chunk, width), BF16),
                 vmem((rows, width), BF16),
                 vmem((rows, width), BF16),
-                vmem((rows, width), BF16),
-                vmem((2, rows, width), BF16),
-                vmem((2, rows, width), BF16),
-                vmem((chunks, chunk, width), BF16),
-                vmem((chunks, chunk, width), BF16),
+                vmem((width, rows), BF16),
+                vmem((2, chunks, width, chunk), BF16),
+                vmem((2, chunks, width, chunk), BF16),
+                vmem((chunks, width, chunk), BF16),
+                vmem((chunks, width, chunk), BF16),
                 vmem((PLANE, part + 16, width), BF16),
                 vmem((PLANE, part + 16, width), BF16),
                 vmem((groups, part + 16, width), BF16),

time: 39.7 us -> 39.7 us (level)
  no operation moved by 1% of the time
where the time goes in v4:
time: 39.7 us; the launch traced here: 39.6 us
  Pallas kernels  38.9 us (98%)
  between operations  0.64 us (2%)
    pallas_call x1, Pallas kernels, local(): pl.pallas_call(functools.partial(kernel, n, 1.0 / math.sqrt(rows * n)), o...  36.9 us
    pallas_call x1, Pallas kernels, local(): pl.pallas_call(hand_out, out_shape=shapes, in_specs=[hbm] * 4, out_specs=...  2.03 us

profile of v4, /device:TPU:0, one launch (start us, length us, event | category | flops | bytes accessed | tf_op | source)
XLA Modules:
  0.0 39.6 jit_solution(10593819372749252642)
XLA Ops:
  0.6 36.9 %shard_map.102 = (bf16[768,256]{1,0:T(8,128)(2,1)}, bf16[768,256]{1,0:T(8,128)(2,1)}, f32[256,256]{1,0:T(8,128)}, f32[1,256]{1,0:T(1,128)}) custom-call(s32[6,6]{1,0:T(8,128)} %cols_hbm.1, s32[1,6]{1,0:T(1,128)} %bitcast.4, bf16[768,256]{1,0:T(8,128)(2,1)} %feat_hbm.1, bf16[6,6,128,128]{3,2,1,0:T(8,128)(2,1)} %tiles_hbm.1, bf16[256,256]{1,0:T(8,128)(2,1)} %w_hbm.1, ...), custom_call_target="tpu_custom_call" | custom-call | tf_op jit(solution)/shard_map/pallas_call | solution.py:395
  37.5 2.0 %shard_map.103 = (bf16[768,256]{1,0:T(8,128)(2,1)}, bf16[768,256]{1,0:T(8,128)(2,1)}, f32[256,256]{1,0:T(8,128)}, f32[1,256]{1,0:T(1,128)}) custom-call(bf16[768,256]{1,0:T(8,128)(2,1)} %get-tuple-element.12.refs_0_, bf16[768,256]{1,0:T(8,128)(2,1)} %get-tuple-element.13.refs_1_, f32[256,256]{1,0:T(8,128)} %get-tuple-element.14.refs_2_, ...), custom_call_target="tpu_custom_call" | custom-call | tf_op jit(solution)/shard_map/pallas_call | solution.py:444

commit v5 on v4

--- a/solution.py
+++ b/solution.py
@@ -178,12 +178,32 @@
         return jnp.where(even, chunks - 1 - j, j)
 
     for j in range(chunks):
-        @pl.when(has_far if j < chunks - 1 else far_even)
+        at = chunk_at(forward_chunk(j))
+
+        def add_far(reach):
+            p_send[j] = (acc[at, :] + dot(band[at, :reach], feat[:reach])).astype(BF16)
+
+        @pl.when(far_even)
         def _():
             far_feat(j).wait_recv()
 
-        at, reach = chunk_at(forward_chunk(j)), (j + 1) * chunk
-        p_send[j] = (acc[at, :] + dot(band[at, :reach], feat[:reach])).astype(BF16)
+        @pl.when(even)
+        def _():
+            add_far((j + 1) * chunk)
+
+        if j == 0:
+            @pl.when(jnp.logical_not(even))
+            def _():
+                p_send[j] = acc[at, :].astype(BF16)
+        else:
+            @pl.when(far_odd)
+            def _():
+                far_feat(j - 1).wait_recv()
+
+            @pl.when(jnp.logical_not(even))
+            def _():
+                add_far(j * chunk)
+
         p_copy(j).start()
 
     for load in loads[4:]:
@@ -306,14 +326,14 @@
             acc_t[m] + s_recv[0, j].astype(F32) + s_recv[1, m].astype(F32)
         ).astype(BF16)
         t_copy(j).start()
-        if j == 1:
+        if j == 2:
             for d in range(1, PLANE):
                 w_copy(d, lax.rem(quad + PLANE - d, PLANE)).wait_recv()
             z_recv[layer] = sum(w_recv[c].astype(F32) for c in range(PLANE)).astype(BF16)
             for d in range(1, groups):
                 z_copy(d, layer).start()
-        if j == chunks - 2:
-            finish_weight()
+
+    finish_weight()
 
     def fg_out(j):
         at = chunk_at(backward_chunk(j))

time: 39.7 us -> 38.8 us (0.977)
  Pallas kernels: 38.9 us -> 38 us
    pallas_call x1, Pallas kernels: 36.9 us -> 35.9 us  [local(): pl.pallas_call(functools.partial(kernel, n, 1.0 / math.sqrt(rows * n)), o...]
where the time goes in v5:
time: 38.8 us; the launch traced here: 38.6 us
  Pallas kernels  38 us (98%)
  between operations  0.64 us (2%)
    pallas_call x1, Pallas kernels, local(): pl.pallas_call(functools.partial(kernel, n, 1.0 / math.sqrt(rows * n)), o...  35.9 us
    pallas_call x1, Pallas kernels, local(): pl.pallas_call(hand_out, out_shape=shapes, in_specs=[hbm] * 4, out_specs=...  2.03 us

profile of v5, /device:TPU:0, one launch (start us, length us, event | category | flops | bytes accessed | tf_op | source)
XLA Modules:
  0.0 38.6 jit_solution(10113736721764633805)
XLA Ops:
  0.6 35.9 %shard_map.102 = (bf16[768,256]{1,0:T(8,128)(2,1)}, bf16[768,256]{1,0:T(8,128)(2,1)}, f32[256,256]{1,0:T(8,128)}, f32[1,256]{1,0:T(1,128)}) custom-call(s32[6,6]{1,0:T(8,128)} %cols_hbm.1, s32[1,6]{1,0:T(1,128)} %bitcast.4, bf16[768,256]{1,0:T(8,128)(2,1)} %feat_hbm.1, bf16[6,6,128,128]{3,2,1,0:T(8,128)(2,1)} %tiles_hbm.1, bf16[256,256]{1,0:T(8,128)(2,1)} %w_hbm.1, ...), custom_call_target="tpu_custom_call" | custom-call | tf_op jit(solution)/shard_map/pallas_call | solution.py:415
  36.6 2.0 %shard_map.103 = (bf16[768,256]{1,0:T(8,128)(2,1)}, bf16[768,256]{1,0:T(8,128)(2,1)}, f32[256,256]{1,0:T(8,128)}, f32[1,256]{1,0:T(1,128)}) custom-call(bf16[768,256]{1,0:T(8,128)(2,1)} %get-tuple-element.12.refs_0_, bf16[768,256]{1,0:T(8,128)(2,1)} %get-tuple-element.13.refs_1_, f32[256,256]{1,0:T(8,128)} %get-tuple-element.14.refs_2_, ...), custom_call_target="tpu_custom_call" | custom-call | tf_op jit(solution)/shard_map/pallas_call | solution.py:464

commit v6 on v5

--- a/solution.py
+++ b/solution.py
@@ -40,7 +40,6 @@
     quad = lax.rem(me, PLANE)
     layer = lax.div(me, PLANE)
     chunk, chunks = tile, nb
-    bulk = 2 * tile
     even = lax.rem(me, 2) == 0
     near = jnp.where(even, me + 1, me - 1)
     far = jnp.where(even, me - 1, me + 1)
@@ -160,16 +159,7 @@
     def chunk_at(m):
         return pl.ds(pl.multiple_of(m * chunk, chunk), chunk)
 
-    def bulk_at(m):
-        return pl.ds(pl.multiple_of(m * bulk, bulk), bulk)
-
     near_feat.wait_recv()
-
-    def near_rows(m, carry):
-        acc[bulk_at(m), :] = dot(band[bulk_at(m), rows:], feat[rows:])
-        return carry
-
-    lax.fori_loop(0, rows // bulk, near_rows, 0)
 
     def p_copy(j):
         return remote(p_send.at[j], p_recv.at[j], p_ssem.at[j], p_rsem.at[j], partner)
@@ -179,9 +169,10 @@
 
     for j in range(chunks):
         at = chunk_at(forward_chunk(j))
+        acc[...] = dot(band[at, rows:], feat[rows:])
 
         def add_far(reach):
-            p_send[j] = (acc[at, :] + dot(band[at, :reach], feat[:reach])).astype(BF16)
+            p_send[j] = (acc[...] + dot(band[at, :reach], feat[:reach])).astype(BF16)
 
         @pl.when(far_even)
         def _():
@@ -194,7 +185,7 @@
         if j == 0:
             @pl.when(jnp.logical_not(even))
             def _():
-                p_send[j] = acc[at, :].astype(BF16)
+                p_send[j] = acc[...].astype(BF16)
         else:
             @pl.when(far_odd)
             def _():
@@ -431,7 +422,7 @@
                 vmem((rows, 3 * rows), BF16),
                 vmem((rows, width), BF16),
                 pltpu.SMEM((nb * slots,), jnp.int32),
-                vmem((rows, width), F32),
+                vmem((chunk, width), F32),
                 vmem((chunks, width, chunk), F32),
                 vmem((chunks, chunk, width), BF16),
                 vmem((chunks, chunk, width), BF16),

time: 38.8 us -> 38 us (0.979)
  Pallas kernels: 38 us -> 37 us
    pallas_call x1, Pallas kernels: 35.9 us -> 35 us  [local(): pl.pallas_call(functools.partial(kernel, n, 1.0 / math.sqrt(rows * n)), o...]
where the time goes in v6:
time: 38 us; the launch traced here: 37.7 us
  Pallas kernels  37 us (97%)
  between operations  0.64 us (2%)
    pallas_call x1, Pallas kernels, local(): pl.pallas_call(functools.partial(kernel, n, 1.0 / math.sqrt(rows * n)), o...  35 us
    pallas_call x1, Pallas kernels, local(): pl.pallas_call(hand_out, out_shape=shapes, in_specs=[hbm] * 4, out_specs=...  2.03 us

profile of v6, /device:TPU:0, one launch (start us, length us, event | category | flops | bytes accessed | tf_op | source)
XLA Modules:
  0.0 37.7 jit_solution(12594103133467520977)
XLA Ops:
  0.6 35.0 %shard_map.102 = (bf16[768,256]{1,0:T(8,128)(2,1)}, bf16[768,256]{1,0:T(8,128)(2,1)}, f32[256,256]{1,0:T(8,128)}, f32[1,256]{1,0:T(1,128)}) custom-call(s32[6,6]{1,0:T(8,128)} %cols_hbm.1, s32[1,6]{1,0:T(1,128)} %bitcast.4, bf16[768,256]{1,0:T(8,128)(2,1)} %feat_hbm.1, bf16[6,6,128,128]{3,2,1,0:T(8,128)(2,1)} %tiles_hbm.1, bf16[256,256]{1,0:T(8,128)(2,1)} %w_hbm.1, ...), custom_call_target="tpu_custom_call" | custom-call | tf_op jit(solution)/shard_map/pallas_call | solution.py:406
  35.7 2.0 %shard_map.103 = (bf16[768,256]{1,0:T(8,128)(2,1)}, bf16[768,256]{1,0:T(8,128)(2,1)}, f32[256,256]{1,0:T(8,128)}, f32[1,256]{1,0:T(1,128)}) custom-call(bf16[768,256]{1,0:T(8,128)(2,1)} %get-tuple-element.12.refs_0_, bf16[768,256]{1,0:T(8,128)(2,1)} %get-tuple-element.13.refs_1_, f32[256,256]{1,0:T(8,128)} %get-tuple-element.14.refs_2_, ...), custom_call_target="tpu_custom_call" | custom-call | tf_op jit(solution)/shard_map/pallas_call | solution.py:455
